TPU v7x, 128 devices: a whole 4x4x4 slice. The times are simulated.
128 devices in a mesh: row: 8 (over z, core), col: 16 (over x, y).
Axes of the slice: x: 4, y: 4, z: 4, core: 2. Of those that a mesh axis runs over, the one named last changes fastest.
Arguments:
- acts: bfloat16 [1024, 12288], P('col', 'row'), may hold values from -6 to 6
- up_weight: bfloat16 [12288, 49152], P('row', 'col'), may hold values from -0.0546875 to 0.0546875
- out_grad: bfloat16 [1024, 49152], P('row', 'col'), may hold values from -6 to 6
Outputs:
- input_grad: bfloat16 [1024, 12288], P('col', 'row')
- weight_grad: bfloat16 [12288, 49152], P('row', 'col')
All inputs are finite; a program needn't handle non-finite values.
Results may differ from a plain program's by a relative error of at most 0.023.
Values may be sent and summed in bfloat16 or wider, within the bound.
A program may use at most 128 MiB of HBM per device.

v0:
```python
import jax
import jax.numpy as jnp
from jax import lax
from jax.sharding import PartitionSpec as P


def gelu_slope(pre):
    cdf = 0.5 * (1.0 + lax.erf(pre * 0.7071067811865476))
    dens = jnp.exp(-0.5 * pre * pre) * 0.3989422804014327
    return cdf + pre * dens


def per_device(acts, up_weight, out_grad):
    all_acts = lax.all_gather(acts, "col", axis=0, tiled=True)
    part_rows = all_acts
    pre_local = lax.psum_scatter(
        jnp.dot(part_rows, up_weight, preferred_element_type=jnp.float32).astype(jnp.bfloat16),
        "row",
        scatter_dimension=0,
        tiled=True,
    ).astype(jnp.float32)
    local_grad = (out_grad.astype(jnp.float32) * gelu_slope(pre_local)).astype(jnp.bfloat16)
    hidden_grad = lax.all_gather(local_grad, "row", axis=0, tiled=True)
    part_rows = hidden_grad
    input_grad = lax.psum_scatter(
        lax.dot_general(
            part_rows, up_weight, (((1,), (1,)), ((), ())), preferred_element_type=jnp.float32
        ).astype(jnp.bfloat16),
        "col",
        scatter_dimension=0,
        tiled=True,
    )
    weight_grad = lax.dot_general(
        all_acts, hidden_grad, (((0,), (0,)), ((), ())), preferred_element_type=jnp.float32
    ).astype(jnp.bfloat16)
    return (input_grad, weight_grad)


def solution(mesh):
    in_specs = (P("col", "row"), P("row", "col"), P("row", "col"))
    out_specs = (P("col", "row"), P("row", "col"))
    return jax.shard_map(
        per_device, mesh=mesh, in_specs=in_specs, out_specs=out_specs, check_vma=False
    )
```

profile of v0, /device:TPU:2, one launch (start us, length us, event | category | flops | bytes accessed | tf_op | source)
XLA Modules:
  0.0 258.5 jit_solution(3975695777644736077)
XLA Ops:
  7.2 0.0 all-gather.3.cloned.1.call-start
  7.2 0.7 all-gather.3.cloned.1.call-update
  7.9 0.0 reduce-scatter.3.cloned.1.call-start
  7.9 51.7 %all-gather.3.cloned.1.call-done = bf16[1024,1536]{1,0:T(8,128)(2,1)} async-done(((bf16[64,1536]{1,0:T(8,128)(2,1)}), bf16[1024,1536]{1,0:T(8,128)(2,1)}) %all-gather.3.cloned.1.call-update) | async-done | bytes 3145744 | tf_op jit(solution)/shard_map/all_gather | solution.py:14
  59.6 15.1 %convolution_convert_fusion.1 = bf16[1024,3072]{1,0:T(8,128)(2,1)} fusion(bf16[1024,1536]{1,0:T(8,128)(2,1)} %all-gather.3.cloned.1.call-done, bf16[1536,3072]{1,0:T(8,128)(2,1)} %param.4), kind=kOutput, calls=%fused_computation.2 | convolution fusion | flops 9666822144 | bytes 18874368 | tf_op jit(solution)/shard_map/dot_general | solution.py:17
  74.7 0.0 copy-start
  74.7 0.0 reduce-scatter.3.cloned.1.call-update
  74.7 0.0 all-gather.5.cloned.1.call-start
  74.8 42.5 %reduce-scatter.3.cloned.1.call-done = bf16[128,3072]{1,0:T(8,128)(2,1)} async-done(((bf16[1024,3072]{1,0:T(8,128)(2,1)}), bf16[128,3072]{1,0:T(8,128)(2,1)}) %reduce-scatter.3.cloned.1.call-update) | async-done | bytes 786448 | tf_op jit(solution)/shard_map/reduce_scatter | solution.py:16
  117.3 0.0 copy-done
  117.3 2.8 %fusion.8 = bf16[128,3072]{1,0:T(8,128)(2,1)} fusion(bf16[128,3072]{1,0:T(8,128)(2,1)} %reduce-scatter.3.cloned.1.call-done, bf16[128,3072]{1,0:T(8,128)(2,1)S(1)} %copy-done), kind=kLoop, calls=%fused_computation.15 | loop fusion | flops 4718592 | bytes 2359296 | tf_op jit(solution)/shard_map/convert_element_type | solution.py:22
  120.0 0.0 all-gather.5.cloned.1.call-update
  120.1 0.0 reduce-scatter.5.cloned.1.call-start
  120.1 40.8 %all-gather.5.cloned.1.call-done = bf16[1024,3072]{1,0:T(8,128)(2,1)} async-done(((bf16[128,3072]{1,0:T(8,128)(2,1)}), bf16[1024,3072]{1,0:T(8,128)(2,1)}) %all-gather.5.cloned.1.call-update) | async-done | bytes 6291472 | tf_op jit(solution)/shard_map/all_gather | solution.py:23
  160.9 15.6 %convolution_convert_fusion.2 = bf16[1024,1536]{1,0:T(8,128)(2,1)} fusion(bf16[1024,3072]{1,0:T(8,128)(2,1)} %all-gather.5.cloned.1.call-done, bf16[1536,3072]{1,0:T(8,128)(2,1)} %param.4), kind=kOutput, calls=%fused_computation.3 | convolution fusion | flops 9665249280 | bytes 18874368 | tf_op jit(solution)/shard_map/dot_general | solution.py:26
  176.6 0.0 copy-start.1
  176.6 0.0 reduce-scatter.5.cloned.1.call-update
  176.6 1.9 copy-done.1
  178.5 14.9 %fusion = bf16[1536,3072]{0,1:T(8,128)(2,1)} fusion(bf16[1024,3072]{1,0:T(8,128)(2,1)} %all-gather.5.cloned.1.call-done, bf16[1024,1536]{1,0:T(8,128)(2,1)S(1)} %copy-done.1), kind=kOutput, calls=%fused_computation.1 | convolution fusion | flops 9668395008 | bytes 18874368 | tf_op jit(solution)/shard_map/dot_general | solution.py:33
  193.4 12.6 %copy.5 = bf16[1536,3072]{1,0:T(8,128)(2,1)} copy(bf16[1536,3072]{0,1:T(8,128)(2,1)} %fusion) | data formatting | bytes 18874368
  206.0 46.0 %reduce-scatter.5.cloned.1.call-done = bf16[64,1536]{1,0:T(8,128)(2,1)} async-done(((bf16[1024,1536]{1,0:T(8,128)(2,1)}), bf16[64,1536]{1,0:T(8,128)(2,1)}) %reduce-scatter.5.cloned.1.call-update) | async-done | bytes 196624 | tf_op jit(solution)/shard_map/reduce_scatter | solution.py:25
Async XLA Ops:
  7.2 52.5 %all-gather.3.cloned.1.call-start = ((), (), s32[]{:S(2)}) async-start(), calls=%async_computation.2 | async-start | bytes 3342336 | tf_op jit(solution)/shard_map/all_gather | solution.py:14
  7.9 109.4 %reduce-scatter.3.cloned.1.call-start = ((), (), s32[]{:S(2)}) async-start(), calls=%async_computation.3 | async-start | bytes 7077888 | tf_op jit(solution)/shard_map/reduce_scatter | solution.py:16
  74.7 42.6 %copy-start = (bf16[128,3072]{1,0:T(8,128)(2,1)S(1)}, bf16[128,3072]{1,0:T(8,128)(2,1)}, u32[]{:S(2)}) copy-start(bf16[128,3072]{1,0:T(8,128)(2,1)} %param.5) | copy-start | bytes 2359300
  74.7 86.2 %all-gather.5.cloned.1.call-start = ((), (), s32[]{:S(2)}) async-start(), calls=%async_computation.4 | async-start | bytes 7077888 | tf_op jit(solution)/shard_map/all_gather | solution.py:23
  120.1 131.9 %reduce-scatter.5.cloned.1.call-start = ((), (), s32[]{:S(2)}) async-start(), calls=%async_computation.5 | async-start | bytes 3342336 | tf_op jit(solution)/shard_map/reduce_scatter | solution.py:25
  176.6 1.9 copy-start.1
Sparse Core Ops, SparseCore 0:
  10.2 49.4 all-gather.2
  74.9 42.3 reduce-scatter.2
  120.2 40.6 all-gather.4
  176.7 75.2 reduce-scatter.4
where the time goes:
time: 260 us; the launch traced here: 259 us
  waiting for transfers between devices  182 us (70%)
  matrix products  45.6 us (18%)
  local copies, waits for them, and re-layouts  14.5 us (6%)
  between operations  13.8 us (5%)
  other arithmetic  2.75 us (1%)
    all_gather x1, waiting for transfers between devices, per_device(): all_acts = lax.all_gather(acts, 'col', axis=0, tiled=True)  51.7 us
    reduce_scatter x1, waiting for transfers between devices, per_device(): lax.psum_scatter(lax.dot_general(part_rows, up_weight, (((1,), (1,)), (()...  46 us
    reduce_scatter x1, waiting for transfers between devices, per_device(): lax.psum_scatter(jnp.dot(part_rows, up_weight, preferred_element_type=jnp...  42.5 us
    all_gather x1, waiting for transfers between devices, per_device(): hidden_grad = lax.all_gather(local_grad, 'row', axis=0, tiled=True)  40.8 us
    dot_general x1, matrix products, per_device(): lax.dot_general(part_rows, up_weight, (((1,), (1,)), ((), ())), preferred...  15.6 us
    dot_general x1, matrix products, per_device(): jnp.dot(part_rows, up_weight, preferred_element_type=jnp.float32)  15.1 us
    dot_general x1, matrix products, per_device(): lax.dot_general(all_acts, hidden_grad, (((0,), (0,)), ((), ())), preferre...  14.9 us
    unnamed x5, local copies, waits for them, and re-layouts  14.5 us
  transfers between devices with their start and end apart: 4, of which 4 were waited for; matrix products, arithmetic and copies ran while one was open for 11% of the time, Pallas kernels for 0%

commit v1 on v0

v1 whole, which is shorter than its diff:
```python
import functools

import jax
import jax.numpy as jnp
from jax import lax
from jax.experimental import pallas as pl
from jax.experimental.pallas import tpu as pltpu
from jax.sharding import PartitionSpec as P

F32, BF16 = jnp.float32, jnp.bfloat16
MESH = pl.DeviceIdType.MESH
N_SEMS = 128


def gelu_slope(pre):
    cdf = 0.5 * (1.0 + lax.erf(pre * 0.7071067811865476))
    dens = jnp.exp(-0.5 * pre * pre) * 0.3989422804014327
    return cdf + pre * dens


def tile_of(size, want):
    return want if size % want == 0 else size


def kernel(
    acts_ref, w_ref, og_ref, ig_ref, wg_ref,
    acts, w, og, acts_t, part, sib_in, z_in_m, z_in_p, hidden, ig, y_in_m, y_in_p, xs, x_in_m, x_in_p,
    local_sem, send_sem, recv_sem,
):
    tb, feats = acts_ref.shape
    ob, hid = og_ref.shape
    half, quarter = ob // 2, ob // 4
    grp = 4 * tb
    tn = tile_of(hid, 512)
    tf = tile_of(feats, 512)
    tm = tile_of(feats, 256)

    row, col = lax.axis_index("row"), lax.axis_index("col")
    z, k = lax.div(row, 2), lax.rem(row, 2)
    x, y = lax.div(col, 4), lax.rem(col, 4)
    nxt = lambda v, by: lax.rem(v + by, 4)
    sib = {"row": z * 2 + (1 - k)}
    zp, zm = {"row": nxt(z, 1) * 2 + k}, {"row": nxt(z, 3) * 2 + k}
    xp, xm = {"col": nxt(x, 1) * 4 + y}, {"col": nxt(x, 3) * 4 + y}
    yp, ym = {"col": x * 4 + nxt(y, 1)}, {"col": x * 4 + nxt(y, 3)}

    sent = []

    def send(src, dst, to):
        i = len(sent)
        copy = pltpu.make_async_remote_copy(
            src_ref=src, dst_ref=dst, send_sem=send_sem.at[i], recv_sem=recv_sem.at[i],
            device_id=to, device_id_type=MESH,
        )
        copy.start()
        sent.append(copy)
        return copy

    def at(ref, start, size):
        return ref.at[pl.ds(pl.multiple_of(start, size), size)]

    barrier = pltpu.get_barrier_semaphore()
    for to in (sib, zp, zm, xp, xm, yp, ym):
        pl.semaphore_signal(barrier, inc=1, device_id=to, device_id_type=MESH)
    own_acts = at(acts, (x * 4 + y) * tb, tb)
    load_acts = pltpu.make_async_copy(acts_ref, own_acts, local_sem.at[0])
    load_w = pltpu.make_async_copy(w_ref, w, local_sem.at[1])
    load_og = pltpu.make_async_copy(og_ref, og, local_sem.at[2])
    load_acts.start()
    load_w.start()
    load_og.start()
    load_acts.wait()
    pl.semaphore_wait(barrier, 7)

    hb = tb // 2

    def ag_start(block, to_p, to_m):
        a = lambda by: at(acts, block(by), hb)
        b = lambda by: at(acts, block(by) + hb, hb)
        pa = send(a(0), a(0), to_p)
        mb = send(b(0), b(0), to_m)
        pb = send(b(0), b(0), to_p)
        ma = send(a(0), a(0), to_m)
        return a, b, pa, mb, pb, ma, to_p, to_m

    def ag_forward(state):
        a, b, pa, mb, pb, ma, to_p, to_m = state
        pa.wait_recv()
        fa = send(a(3), a(3), to_p)
        mb.wait_recv()
        fb = send(b(1), b(1), to_m)
        return pb, ma, fa, fb

    def ag_finish(copies):
        for copy in copies:
            copy.wait_recv()

    ag_finish(ag_forward(ag_start(lambda by: (nxt(x, by) * 4 + y) * tb, xp, xm)))
    order = [nxt(z, 2), nxt(z, 1), nxt(z, 3), z]
    y_start = lambda s: ag_start(lambda by: (order[s] * 4 + nxt(y, by)) * tb, yp, ym)

    def dot1(s):
        rows = pl.ds(pl.multiple_of(order[s] * grp, grp), grp)
        theirs = part.at[s, pl.ds(pl.multiple_of((1 - k) * ob, ob), ob)]
        sem = len(sent)

        def tile(n, carry):
            cols = pl.ds(pl.multiple_of(n * tn, tn), tn)
            part[s, :, cols] = jnp.dot(acts[rows, :], w[:, cols], preferred_element_type=F32).astype(BF16)
            pltpu.make_async_remote_copy(
                src_ref=theirs.at[:, cols], dst_ref=sib_in.at[s, :, cols], send_sem=send_sem.at[sem],
                recv_sem=recv_sem.at[sem], device_id=sib, device_id_type=MESH,
            ).start()
            return carry

        lax.fori_loop(0, hid // tn, tile, 0)
        whole = pltpu.make_async_remote_copy(
            src_ref=theirs, dst_ref=sib_in.at[s], send_sem=send_sem.at[sem],
            recv_sem=recv_sem.at[sem], device_id=sib, device_id_type=MESH,
        )
        sent.append(whole)
        return whole

    own_row = pl.multiple_of(k * ob, ob)

    def add_into(dst, dst_row, src, src_row, rows):
        step = min(rows, 32)
        for r in range(0, rows, step):
            def tile(n, carry):
                cols = pl.ds(pl.multiple_of(n * tn, tn), tn)
                into = pl.ds(pl.multiple_of(dst_row + r, step), step)
                total = dst[into, cols].astype(F32) + src[src_row + r:src_row + r + step, cols].astype(F32)
                dst[into, cols] = total.astype(BF16)
                return carry

            lax.fori_loop(0, dst.shape[-1] // tn, tile, 0)

    def core_sum(s, copy):
        copy.wait_recv()
        add_into(part.at[s], own_row, sib_in.at[s], 0, ob)

    mine = lambda s, start, size: part.at[s, pl.ds(pl.multiple_of(own_row + start, size), size)]

    g = ag_forward(y_start(0))
    nx = y_start(1)
    load_w.wait()
    ag_finish(g)
    c = dot1(0)
    g = ag_forward(nx)
    nx = y_start(2)
    core_sum(0, c)
    opp_p = send(mine(0, 0, half), z_in_m.at[0], zp)
    opp_m = send(mine(0, half, half), z_in_p.at[0], zm)
    ag_finish(g)
    c = dot1(1)
    g = ag_forward(nx)
    nx = y_start(3)
    core_sum(1, c)
    dir_p = send(mine(1, half, half), z_in_m.at[1], zp)
    ag_finish(g)
    c = dot1(2)
    g = ag_forward(nx)
    core_sum(2, c)
    dir_m = send(mine(2, 0, half), z_in_p.at[1], zm)
    ag_finish(g)
    c = dot1(3)
    opp_p.wait_recv()
    add_into(part.at[1], own_row, z_in_m.at[0], 0, half)
    acc_p = [send(mine(1, j * quarter, quarter), z_in_m.at[2, pl.ds(j * quarter, quarter)], zp) for j in range(2)]
    opp_m.wait_recv()
    add_into(part.at[2], own_row + half, z_in_p.at[0], 0, half)
    acc_m = [send(mine(2, half + j * quarter, quarter), z_in_p.at[2, pl.ds(j * quarter, quarter)], zm) for j in range(2)]
    core_sum(3, c)
    load_og.wait()

    def turn(n, carry):
        cols = pl.ds(pl.multiple_of(n * tm, tm), tm)
        for t in range(4):
            acts_t[cols, t * grp:(t + 1) * grp] = acts[t * grp:(t + 1) * grp, cols].T
        return carry

    lax.fori_loop(0, feats // tm, turn, 0)

    dir_p.wait_recv()
    dir_m.wait_recv()
    base = lambda zz, kk: zz * 2 * ob + kk * ob
    piece = lambda first, start: at(hidden, first + start, quarter)
    own_base = base(z, k)

    def slope_piece(start, from_m, from_p):
        def tile(n, carry):
            cols = pl.ds(pl.multiple_of(n * tn, tn), tn)
            own = part[3, pl.ds(pl.multiple_of(own_row + start, quarter), quarter), cols]
            pre = own.astype(F32) + from_m[:, cols].astype(F32) + from_p[:, cols].astype(F32)
            grad = og[start:start + quarter, cols].astype(F32) * gelu_slope(pre)
            hidden[pl.ds(pl.multiple_of(own_base + start, quarter), quarter), cols] = grad.astype(BF16)
            return carry

        lax.fori_loop(0, hid // tn, tile, 0)
        here = piece(own_base, start)
        return send(here, here, sib), send(here, here, zp), send(here, here, zm)

    starts = (0, half, quarter, half + quarter)
    own_sends = []
    for j in range(2):
        q = pl.ds(j * quarter, quarter)
        acc_p[j].wait_recv()
        own_sends.append(slope_piece(j * quarter, z_in_m.at[2, q], z_in_p.at[1, q]))
        acc_m[j].wait_recv()
        own_sends.append(slope_piece(half + j * quarter, z_in_m.at[1, q], z_in_p.at[2, q]))

    def dot2(s, g):
        rows = pl.ds(pl.multiple_of(g * grp, grp), grp)

        def tile(n, carry):
            cols = pl.ds(pl.multiple_of(n * tf, tf), tf)
            ig[s, :, cols] = lax.dot_general(
                hidden[rows, :], w[cols, :], (((1,), (1,)), ((), ())), preferred_element_type=F32
            ).astype(BF16)
            return carry

        lax.fori_loop(0, feats // tf, tile, 0)

    def rs_start(src, row_of, in_m, in_p, to_p, to_m):
        blk = lambda by, start: src.at[pl.ds(pl.multiple_of(row_of(by) + start, hb), hb)]
        op = send(blk(2, 0), in_m.at[0], to_p)
        om = send(blk(2, hb), in_p.at[0], to_m)
        dp = send(blk(1, hb), in_m.at[1], to_p)
        dm = send(blk(3, 0), in_p.at[1], to_m)
        return src, row_of, blk, in_m, in_p, to_p, to_m, op, om, dp, dm

    def rs_middle(state):
        src, row_of, blk, in_m, in_p, to_p, to_m, op, om, dp, dm = state
        op.wait_recv()
        add_into(src, row_of(1), in_m.at[0], 0, hb)
        ap = send(blk(1, 0), in_m.at[2], to_p)
        om.wait_recv()
        add_into(src, row_of(3) + hb, in_p.at[0], 0, hb)
        am = send(blk(3, hb), in_p.at[2], to_m)
        return src, row_of, in_m, in_p, (dp, dm, ap, am)

    def rs_finish(state, out):
        src, row_of, in_m, in_p, copies = state
        for copy in copies:
            copy.wait_recv()
        for start, from_m, from_p in ((0, in_m.at[2], in_p.at[1]), (hb, in_m.at[1], in_p.at[2])):
            def tile(n, carry):
                cols = pl.ds(pl.multiple_of(n * tf, tf), tf)
                own = src[pl.ds(pl.multiple_of(row_of(0) + start, hb), hb), cols]
                total = own.astype(F32) + from_m[:, cols].astype(F32) + from_p[:, cols].astype(F32)
                out[start:start + hb, cols] = total.astype(BF16)
                return carry

            lax.fori_loop(0, feats // tf, tile, 0)

    y_rs = lambda s: rs_start(ig.at[s], lambda by: nxt(y, by) * tb, y_in_m.at[s], y_in_p.at[s], yp, ym)

    for s3 in own_sends:
        s3[0].wait_recv()
    dot2(0, z)
    y0 = y_rs(0)

    low, high = nxt(z, 3), nxt(z, 1)
    to_sib, fwd_p, fwd_m = [], [], []
    for n, start in enumerate(starts):
        own_sends[n][1].wait_recv()
        here = piece(base(low, k), start)
        if start < half:
            fwd_p.append(send(here, here, zp))
        to_sib.append(send(here, here, sib))
        own_sends[n][2].wait_recv()
        here = piece(base(high, k), start)
        if start >= half:
            fwd_m.append(send(here, here, zm))
        to_sib.append(send(here, here, sib))
    y0 = rs_middle(y0)
    for copy in to_sib:
        copy.wait_recv()
    dot2(1, low)
    y1 = y_rs(1)
    dot2(2, high)
    y2 = y_rs(2)
    rs_finish(y0, xs.at[z])
    y1 = rs_middle(y1)

    opp = nxt(z, 2)
    to_sib = []
    for j in range(2):
        fwd_p[j].wait_recv()
        here = piece(base(opp, k), j * quarter)
        to_sib.append(send(here, here, sib))
        fwd_m[j].wait_recv()
        here = piece(base(opp, k), half + j * quarter)
        to_sib.append(send(here, here, sib))
    y2 = rs_middle(y2)
    for copy in to_sib:
        copy.wait_recv()
    dot2(3, opp)
    y3 = y_rs(3)
    rs_finish(y1, xs.at[low])
    rs_finish(y2, xs.at[high])

    def dot3(m):
        rows = pl.ds(m * tm, tm)

        def tile(n, carry):
            cols = pl.ds(pl.multiple_of(n * tn, tn), tn)
            w[rows, cols] = jnp.dot(acts_t[rows, :], hidden[:, cols], preferred_element_type=F32).astype(BF16)
            return carry

        lax.fori_loop(0, hid // tn, tile, 0)
        out = pltpu.make_async_copy(w.at[rows], wg_ref.at[rows], local_sem.at[3 + m])
        out.start()
        return out

    blocks = feats // tm
    stores = []
    stages = [None] * blocks
    stores.append(dot3(0))
    y3 = rs_middle(y3)
    for m in range(1, min(3, blocks)):
        stores.append(dot3(m))
    rs_finish(y3, xs.at[opp])
    xr = rs_start(
        xs.reshape(4 * tb, feats), lambda by: nxt(x, by) * tb, x_in_m, x_in_p, xp, xm
    )
    for m in range(3, min(4, blocks)):
        stores.append(dot3(m))
    xr = rs_middle(xr)
    for m in range(4, blocks):
        stores.append(dot3(m))
    rs_finish(xr, ig_ref)

    for copy in sent:
        copy.wait_send()
    for out in stores:
        out.wait()


def per_device(acts, up_weight, out_grad):
    tb, feats = acts.shape
    ob, hid = out_grad.shape
    tokens = 16 * tb
    hb, half = tb // 2, ob // 2
    vmem = lambda *shape: pltpu.VMEM(shape, BF16)
    anywhere = pl.BlockSpec(memory_space=pl.ANY)
    flops = 3 * 2 * tokens * feats * hid
    input_grad, weight_grad = pl.pallas_call(
        kernel,
        out_shape=(
            jax.ShapeDtypeStruct((tb, feats), BF16),
            jax.ShapeDtypeStruct((feats, hid), BF16),
        ),
        in_specs=[anywhere] * 3,
        out_specs=(pl.BlockSpec(memory_space=pltpu.VMEM), anywhere),
        scratch_shapes=[
            vmem(tokens, feats),
            vmem(feats, hid),
            vmem(ob, hid),
            vmem(feats, tokens),
            vmem(4, 2 * ob, hid),
            vmem(4, ob, hid),
            vmem(3, half, hid),
            vmem(3, half, hid),
            vmem(tokens, hid),
            vmem(4, 4 * tb, feats),
            vmem(4, 3, hb, feats),
            vmem(4, 3, hb, feats),
            vmem(4, tb, feats),
            vmem(3, hb, feats),
            vmem(3, hb, feats),
            pltpu.SemaphoreType.DMA((16,)),
            pltpu.SemaphoreType.DMA((N_SEMS,)),
            pltpu.SemaphoreType.DMA((N_SEMS,)),
        ],
        compiler_params=pltpu.CompilerParams(
            collective_id=0, has_side_effects=True, vmem_limit_bytes=60 * 2**20
        ),
        cost_estimate=pl.CostEstimate(flops=flops, bytes_accessed=4 * feats * hid, transcendentals=2 * ob * hid),
    )(acts, up_weight, out_grad)
    return input_grad, weight_grad


def solution(mesh):
    in_specs = (P("col", "row"), P("row", "col"), P("row", "col"))
    out_specs = (P("col", "row"), P("row", "col"))
    return jax.shard_map(
        per_device, mesh=mesh, in_specs=in_specs, out_specs=out_specs, check_vma=False
    )
```

time: 260 us -> 134 us (0.52)
  the two profiles are of different devices: /device:TPU:2 before, /device:TPU:0 now
where the time goes in v1:
time: 134 us
  Pallas kernels  123 us (92%)
  local copies, waits for them, and re-layouts  9.89 us (7%)
    pallas_call x1, Pallas kernels, per_device(): pl.pallas_call(kernel, out_shape=(jax.ShapeDtypeStruct((tb, feats), BF16)...  123 us
    unnamed x2, local copies, waits for them, and re-layouts  9.89 us

profile of v1, /device:TPU:0, one launch (start us, length us, event | category | flops | bytes accessed | tf_op | source)
XLA Modules:
  0.0 133.6 jit_solution(7447767539200688623)
XLA Ops:
  0.6 123.1 %shard_map.50 = (bf16[64,1536]{1,0:T(8,128)(2,1)}, bf16[1536,3072]{1,0:T(8,128)(2,1)}) custom-call(bf16[64,1536]{1,0:T(8,128)(2,1)} %acts_ref.1, bf16[1536,3072]{1,0:T(8,128)(2,1)} %w_ref.1, bf16[128,3072]{1,0:T(8,128)(2,1)} %og_ref.1), custom_call_target="tpu_custom_call" | custom-call | flops 28991029248 | bytes 18874368 | tf_op jit(solution)/shard_map/pallas_call | solution.py:348
  123.7 1.6 %copy.7 = bf16[64,1536]{1,0:T(8,128)(2,1)} copy(bf16[64,1536]{1,0:T(8,128)(2,1)} %get-tuple-element.4) | data formatting | bytes 393216
  125.4 8.3 %copy.8 = bf16[1536,3072]{1,0:T(8,128)(2,1)} copy(bf16[1536,3072]{1,0:T(8,128)(2,1)} %get-tuple-element.5) | data formatting | bytes 18874368

commit v2 on v1

v2 whole, which is shorter than its diff:
```python
import functools

import jax
import jax.numpy as jnp
from jax import lax
from jax.experimental import pallas as pl
from jax.experimental.pallas import tpu as pltpu
from jax.sharding import PartitionSpec as P

F32, BF16 = jnp.float32, jnp.bfloat16
MESH = pl.DeviceIdType.MESH
N_SEMS = 144


def gelu_slope(pre):
    cdf = 0.5 * (1.0 + lax.erf(pre * 0.7071067811865476))
    dens = jnp.exp(-0.5 * pre * pre) * 0.3989422804014327
    return cdf + pre * dens


def tile_of(size, want):
    return want if size % want == 0 else size


def kernel(
    acts_ref, w_ref, og_ref, ig_ref, wg_ref,
    acts, w, og, acts_t, part, sib_in, z_in_m, z_in_p, hidden, ig, y_in_m, y_in_p, xs, x_in,
    local_sem, send_sem, recv_sem,
):
    tb, feats = acts_ref.shape
    ob, hid = og_ref.shape
    half, quarter = ob // 2, ob // 4
    grp = 4 * tb
    tn = tile_of(hid // 2, 512)
    tf = tile_of(feats, 512)
    tm = tile_of(feats, 256)

    row, col = lax.axis_index("row"), lax.axis_index("col")
    z, k = lax.div(row, 2), lax.rem(row, 2)
    x, y = lax.div(col, 4), lax.rem(col, 4)
    nxt = lambda v, by: lax.rem(v + by, 4)
    sib = {"row": z * 2 + (1 - k)}
    zp, zm = {"row": nxt(z, 1) * 2 + k}, {"row": nxt(z, 3) * 2 + k}
    xp, xm = {"col": nxt(x, 1) * 4 + y}, {"col": nxt(x, 3) * 4 + y}
    yp, ym = {"col": x * 4 + nxt(y, 1)}, {"col": x * 4 + nxt(y, 3)}

    sent = []

    def ready(src, dst, to):
        i = len(sent)
        sent.append(None)
        return pltpu.make_async_remote_copy(
            src_ref=src, dst_ref=dst, send_sem=send_sem.at[i], recv_sem=recv_sem.at[i],
            device_id=to, device_id_type=MESH,
        )

    def send(src, dst, to):
        copy = ready(src, dst, to)
        copy.start()
        sent[-1] = copy
        return copy

    def at(ref, start, size):
        return ref.at[pl.ds(pl.multiple_of(start, size), size)]

    barrier = pltpu.get_barrier_semaphore()
    for to in (sib, zp, zm, xp, xm, yp, ym):
        pl.semaphore_signal(barrier, inc=1, device_id=to, device_id_type=MESH)
    own_acts = at(acts, (x * 4 + y) * tb, tb)
    load_acts = pltpu.make_async_copy(acts_ref, own_acts, local_sem.at[0])
    load_w = pltpu.make_async_copy(w_ref, w, local_sem.at[1])
    load_og = pltpu.make_async_copy(og_ref, og, local_sem.at[2])
    load_acts.start()
    load_w.start()
    load_og.start()
    load_acts.wait()
    pl.semaphore_wait(barrier, 7)

    hb = tb // 2

    def ag_start(block, to_p, to_m):
        a = lambda by: at(acts, block(by), hb)
        b = lambda by: at(acts, block(by) + hb, hb)
        pa = send(a(0), a(0), to_p)
        mb = send(b(0), b(0), to_m)
        pb = send(b(0), b(0), to_p)
        ma = send(a(0), a(0), to_m)
        return a, b, pa, mb, pb, ma, to_p, to_m

    def ag_forward(state):
        a, b, pa, mb, pb, ma, to_p, to_m = state
        pa.wait_recv()
        fa = send(a(3), a(3), to_p)
        mb.wait_recv()
        fb = send(b(1), b(1), to_m)
        return pb, ma, fa, fb

    def ag_finish(copies):
        for copy in copies:
            copy.wait_recv()

    ag_finish(ag_forward(ag_start(lambda by: (nxt(x, by) * 4 + y) * tb, xp, xm)))
    order = [nxt(z, 2), nxt(z, 1), nxt(z, 3), z]
    y_gather = lambda s: ag_start(lambda by: (order[s] * 4 + nxt(y, by)) * tb, yp, ym)

    def dot1(s, lo=0, hi=hid):
        rows = pl.ds(pl.multiple_of(order[s] * grp, grp), grp)
        theirs = part.at[s, pl.ds(pl.multiple_of((1 - k) * ob, ob), ob)]
        sem = len(sent)

        def to_sib(cols):
            return pltpu.make_async_remote_copy(
                src_ref=theirs.at[:, cols], dst_ref=sib_in.at[s, :, cols], send_sem=send_sem.at[sem],
                recv_sem=recv_sem.at[sem], device_id=sib, device_id_type=MESH,
            )

        def tile(n, carry):
            cols = pl.ds(pl.multiple_of(n * tn, tn), tn)
            part[s, :, cols] = jnp.dot(acts[rows, :], w[:, cols], preferred_element_type=F32).astype(BF16)
            to_sib(cols).start()
            return carry

        lax.fori_loop(lo // tn, hi // tn, tile, 0)
        sent.append(to_sib(pl.ds(lo, hi - lo)))
        return sent[-1]

    own_row = pl.multiple_of(k * ob, ob)

    def add_into(dst, dst_row, src, src_row, rows, lo=0, hi=hid):
        step = min(rows, 32)
        for r in range(0, rows, step):
            def tile(n, carry):
                cols = pl.ds(pl.multiple_of(n * tn, tn), tn)
                into = pl.ds(pl.multiple_of(dst_row + r, step), step)
                total = dst[into, cols].astype(F32) + src[src_row + r:src_row + r + step, cols].astype(F32)
                dst[into, cols] = total.astype(BF16)
                return carry

            lax.fori_loop(lo // tn, hi // tn, tile, 0)

    def core_sum(s, copy, lo=0, hi=hid):
        copy.wait_recv()
        add_into(part.at[s], own_row, sib_in.at[s], 0, ob, lo, hi)

    mine = lambda s, start, size: part.at[s, pl.ds(pl.multiple_of(own_row + start, size), size)]

    g = ag_forward(y_gather(0))
    nx = y_gather(1)
    load_w.wait()
    ag_finish(g)
    opp_p, opp_m = [], []
    for lo, hi in ((0, hid // 2), (hid // 2, hid)):
        c = dot1(0, lo, hi)
        if lo == 0:
            g = ag_forward(nx)
            nx = y_gather(2)
        core_sum(0, c, lo, hi)
        cols = pl.ds(lo, hi - lo)
        opp_p.append(send(mine(0, 0, half).at[:, cols], z_in_m.at[0, :, cols], zp))
        opp_m.append(send(mine(0, half, half).at[:, cols], z_in_p.at[0, :, cols], zm))
    ag_finish(g)
    c = dot1(1)
    g = ag_forward(nx)
    nx = y_gather(3)
    core_sum(1, c)
    dir_p = send(mine(1, half, half), z_in_m.at[1], zp)
    ag_finish(g)
    c = dot1(2)
    g = ag_forward(nx)
    core_sum(2, c)
    dir_m = send(mine(2, 0, half), z_in_p.at[1], zm)
    ag_finish(g)
    c = dot1(3)
    for copy in opp_p:
        copy.wait_recv()
    add_into(part.at[1], own_row, z_in_m.at[0], 0, half)
    acc_p = [send(mine(1, j * quarter, quarter), z_in_m.at[2, pl.ds(j * quarter, quarter)], zp) for j in range(2)]
    for copy in opp_m:
        copy.wait_recv()
    add_into(part.at[2], own_row + half, z_in_p.at[0], 0, half)
    acc_m = [send(mine(2, half + j * quarter, quarter), z_in_p.at[2, pl.ds(j * quarter, quarter)], zm) for j in range(2)]
    core_sum(3, c)
    load_og.wait()

    tokens_of = [
        (z, 0), (z, 1), (nxt(z, 3), 0), (nxt(z, 1), 0),
        (nxt(z, 3), 1), (nxt(z, 1), 1), (nxt(z, 2), 0), (nxt(z, 2), 1),
    ]

    def turn(n, carry):
        cols = pl.ds(pl.multiple_of(n * tm, tm), tm)
        for t, (g, j) in enumerate(tokens_of):
            rows = [at(acts, g * grp + b * tb + j * hb, hb)[:, cols] for b in range(4)]
            acts_t[cols, t * 4 * hb:(t + 1) * 4 * hb] = jnp.concatenate(rows, axis=0).T
        return carry

    lax.fori_loop(0, feats // tm, turn, 0)

    dir_p.wait_recv()
    dir_m.wait_recv()
    piece = lambda zz, kk, q: hidden.at[zz, 2 * kk + q // 2, q % 2]

    def slope_piece(q, from_m, from_p):
        start = q * quarter

        def tile(n, carry):
            cols = pl.ds(pl.multiple_of(n * tn, tn), tn)
            own = part[3, pl.ds(pl.multiple_of(own_row + start, quarter), quarter), cols]
            pre = own.astype(F32) + from_m[:, cols].astype(F32) + from_p[:, cols].astype(F32)
            grad = og[start:start + quarter, cols].astype(F32) * gelu_slope(pre)
            hidden[z, 2 * k + q // 2, q % 2, :, cols] = grad.astype(BF16)
            return carry

        lax.fori_loop(0, hid // tn, tile, 0)
        here = piece(z, k, q)
        return send(here, here, sib), send(here, here, zp), send(here, here, zm)

    arrivals = (0, 2, 1, 3)
    own_sends = {}
    for j in range(2):
        rows = pl.ds(j * quarter, quarter)
        acc_p[j].wait_recv()
        own_sends[j] = slope_piece(j, z_in_m.at[2, rows], z_in_p.at[1, rows])
        acc_m[j].wait_recv()
        own_sends[2 + j] = slope_piece(2 + j, z_in_m.at[1, rows], z_in_p.at[2, rows])

    low, high, opp = nxt(z, 3), nxt(z, 1), nxt(z, 2)

    def dot2(units):
        def tile(n, carry):
            cols = pl.ds(pl.multiple_of(n * tf, tf), tf)
            rows = [hidden[g, :, j].reshape(4 * hb, hid) for _, g, js in units for j in js]
            rows = rows[0] if len(rows) == 1 else jnp.concatenate(rows, axis=0)
            share = lax.dot_general(
                rows, w[cols, :], (((1,), (1,)), ((), ())), preferred_element_type=F32
            ).astype(BF16)
            at_row = 0
            for s, _, js in units:
                for j in js:
                    ig[s, j, :, :, cols] = share[at_row:at_row + 4 * hb].reshape(4, hb, tf)
                    at_row += 4 * hb
            return carry

        lax.fori_loop(0, feats // tf, tile, 0)

    def sum_into(out, terms):
        def tile(n, carry):
            cols = pl.ds(pl.multiple_of(n * tf, tf), tf)
            for p in range(out.shape[0]):
                for q in range(out.shape[1]):
                    total = terms[0][p, q, :, cols].astype(F32)
                    for term in terms[1:]:
                        total = total + term[p, q, :, cols].astype(F32)
                    out[p, q, :, cols] = total.astype(BF16)
            return carry

        lax.fori_loop(0, feats // tf, tile, 0)

    ha, hz = pl.ds(0, hb // 2), pl.ds(hb // 2, hb // 2)

    def y_start(s0, ns, j0, nj):
        ss, js = pl.ds(s0, ns), pl.ds(j0, nj)
        blk = lambda by, rows: ig.at[ss, js, nxt(y, by), rows]
        im = lambda n: y_in_m.at[n, ss, js]
        ip = lambda n: y_in_p.at[n, ss, js]
        op = send(blk(2, ha), im(0), yp)
        om = send(blk(2, hz), ip(0), ym)
        dp = send(blk(1, hz), im(1), yp)
        dm = send(blk(3, ha), ip(1), ym)
        return ss, js, blk, im, ip, op, om, dp, dm

    def y_middle(state):
        ss, js, blk, im, ip, op, om, dp, dm = state
        op.wait_recv()
        sum_into(blk(1, ha), [blk(1, ha), im(0)])
        ap = send(blk(1, ha), im(2), yp)
        om.wait_recv()
        sum_into(blk(3, hz), [blk(3, hz), ip(0)])
        am = send(blk(3, hz), ip(2), ym)
        return ss, js, blk, im, ip, (dp, dm, ap, am)

    def y_finish(state):
        ss, js, blk, im, ip, copies = state
        for copy in copies:
            copy.wait_recv()
        sum_into(xs.at[ss, js, ha], [blk(0, ha), im(2), ip(1)])
        sum_into(xs.at[ss, js, hz], [blk(0, hz), im(1), ip(2)])

    def x_copies(s, g, j0, nj):
        one, js = pl.ds(s, 1), pl.ds(j0, nj)
        mine_x = lambda rows: xs.at[one, js, rows]
        slot = lambda n: x_in.at[n, one, js]
        make = lambda rows, n, to: ready(mine_x(rows), slot(n), to)
        copies = (
            make(ha, 0, xp), make(hz, 1, xm), make(hz, 2, xp), make(ha, 3, xp), make(ha, 4, xm), make(hz, 5, xm)
        )
        return nxt(x, 4 - g), mine_x, slot, copies, (j0, nj)

    def x_start(s, g, j0, nj):
        state = x_copies(s, g, j0, nj)
        away, _, _, copies, _ = state

        @pl.when(away == 2)
        def _():
            copies[0].start()
            copies[1].start()

        @pl.when(away == 3)
        def _():
            copies[2].start()

        @pl.when(away == 1)
        def _():
            copies[4].start()

        return state

    def x_middle(state):
        away, mine_x, slot, copies, _ = state

        @pl.when(away == 3)
        def _():
            copies[0].wait_recv()
            sum_into(mine_x(ha), [mine_x(ha), slot(0)])
            copies[3].start()

        @pl.when(away == 1)
        def _():
            copies[1].wait_recv()
            sum_into(mine_x(hz), [mine_x(hz), slot(1)])
            copies[5].start()

    def x_finish(state):
        away, mine_x, slot, copies, (j0, nj) = state
        result = lambda rows: ig_ref.at[pl.ds(0, 1), pl.ds(j0, nj), rows]

        @pl.when(away == 0)
        def _():
            for n in (2, 3, 4, 5):
                copies[n].wait_recv()
            sum_into(result(ha), [mine_x(ha), slot(3), slot(4)])
            sum_into(result(hz), [mine_x(hz), slot(2), slot(5)])

        for role, used in ((2, (0, 1)), (3, (2, 3)), (1, (4, 5))):
            @pl.when(away == role)
            def _(used=used):
                for n in used:
                    copies[n].wait_send()

    def dot3(m, rows_of, first, later):
        rows = pl.ds(m * tm, tm)
        span = 8 * hb * 2

        def tile(n, carry):
            cols = pl.ds(pl.multiple_of(n * tn, tn), tn)
            units = jnp.concatenate([hidden[g, :, j, :, cols].reshape(4 * hb, tn) for g, j in rows_of], axis=0)
            total = jnp.dot(acts_t[rows, first:first + span], units, preferred_element_type=F32)
            if later:
                total = total + wg_ref[rows, cols].astype(F32)
            wg_ref[rows, cols] = total.astype(BF16)
            return carry

        lax.fori_loop(0, hid // tn, tile, 0)

    blocks = feats // tm

    def early(lo, hi):
        for m in range(lo, hi):
            dot3(m, tokens_of[:4], 0, False)

    def late(lo, hi):
        for m in range(lo, hi):
            dot3(m, tokens_of[4:], 8 * hb * 2, True)

    def neighbours(qs):
        copies = []
        for q in qs:
            own_sends[q][1].wait_recv()
            here = piece(low, k, q)
            if q < 2:
                fwd[q] = send(here, here, zp)
            copies.append(send(here, here, sib))
            own_sends[q][2].wait_recv()
            here = piece(high, k, q)
            if q >= 2:
                fwd[q] = send(here, here, zm)
            copies.append(send(here, here, sib))
        return copies

    def opposite(qs):
        copies = []
        for q in qs:
            fwd[q].wait_recv()
            here = piece(opp, k, q)
            copies.append(send(here, here, sib))
        return copies

    def arrived(copies):
        for copy in copies:
            copy.wait_recv()

    fwd = {}
    arrived([own_sends[q][0] for q in arrivals])
    dot2([(0, z, (0, 1))])
    y0 = y_start(0, 1, 0, 2)
    from_sib = neighbours((0, 2))
    y0 = y_middle(y0)
    arrived(from_sib)
    dot2([(1, low, (0,)), (2, high, (0,))])
    y1 = y_start(1, 2, 0, 1)
    y_finish(y0)
    x0 = x_start(0, z, 0, 2)
    early(0, 2)
    y1 = y_middle(y1)
    x_middle(x0)
    early(2, blocks)
    y_finish(y1)
    from_sib = neighbours((1, 3))
    x_finish(x0)
    arrived(from_sib)
    dot2([(1, low, (1,)), (2, high, (1,))])
    y2 = y_start(1, 2, 1, 1)
    from_sib = opposite((0, 2))
    y2 = y_middle(y2)
    arrived(from_sib)
    dot2([(3, opp, (0,))])
    y3 = y_start(3, 1, 0, 1)
    y_finish(y2)
    x1 = x_start(1, low, 0, 2)
    x2 = x_start(2, high, 0, 2)
    from_sib = opposite((1, 3))
    y3 = y_middle(y3)
    arrived(from_sib)
    dot2([(3, opp, (1,))])
    y4 = y_start(3, 1, 1, 1)
    x_middle(x1)
    x_middle(x2)
    y_finish(y3)
    x3 = x_start(3, opp, 0, 1)
    late(0, 1)
    y4 = y_middle(y4)
    x_middle(x3)
    late(1, 2)
    y_finish(y4)
    x4 = x_start(3, opp, 1, 1)
    late(2, 3)
    x_middle(x4)
    x_finish(x1)
    x_finish(x2)
    x_finish(x3)
    late(3, blocks)
    x_finish(x4)

    for copy in sent:
        if copy is not None:
            copy.wait_send()


def write_out(ig_ref, wg_ref, ig_out, wg_out, sem):
    rows = wg_ref.shape[0] // 4
    copies = [pltpu.make_async_copy(ig_ref, ig_out, sem.at[4])]
    for n in range(4):
        part = pl.ds(n * rows, rows)
        copies.append(pltpu.make_async_copy(wg_ref.at[part], wg_out.at[part], sem.at[n]))
    for copy in copies:
        copy.start()
    for copy in copies:
        copy.wait()


def per_device(acts, up_weight, out_grad):
    tb, feats = acts.shape
    ob, hid = out_grad.shape
    tokens = 16 * tb
    hb, half = tb // 2, ob // 2
    vmem = lambda *shape: pltpu.VMEM(shape, BF16)
    in_hbm = pl.BlockSpec(memory_space=pltpu.HBM)
    in_vmem = pl.BlockSpec(memory_space=pltpu.VMEM)
    flops = 3 * 2 * tokens * feats * hid
    acts, up_weight, out_grad = (
        pltpu.with_memory_space_constraint(a, pltpu.HBM) for a in (acts, up_weight, out_grad)
    )
    input_grad, weight_grad = pl.pallas_call(
        kernel,
        out_shape=(
            vmem(1, 2, hb, feats),
            vmem(feats, hid),
        ),
        in_specs=[in_hbm] * 3,
        out_specs=(in_vmem, in_vmem),
        scratch_shapes=[
            vmem(tokens, feats),
            vmem(feats, hid),
            vmem(ob, hid),
            vmem(feats, tokens),
            vmem(4, 2 * ob, hid),
            vmem(4, ob, hid),
            vmem(3, half, hid),
            vmem(3, half, hid),
            vmem(4, 4, 2, hb, hid),
            vmem(4, 2, 4, hb, feats),
            vmem(3, 4, 2, hb // 2, feats),
            vmem(3, 4, 2, hb // 2, feats),
            vmem(4, 2, hb, feats),
            vmem(6, 4, 2, hb // 2, feats),
            pltpu.SemaphoreType.DMA((3,)),
            pltpu.SemaphoreType.DMA((N_SEMS,)),
            pltpu.SemaphoreType.DMA((N_SEMS,)),
        ],
        compiler_params=pltpu.CompilerParams(
            collective_id=0, has_side_effects=True, vmem_limit_bytes=44 * 2**20
        ),
        cost_estimate=pl.CostEstimate(flops=flops, bytes_accessed=4 * feats * hid, transcendentals=2 * ob * hid),
    )(acts, up_weight, out_grad)
    return pl.pallas_call(
        write_out,
        out_shape=(
            jax.ShapeDtypeStruct((tb, feats), BF16),
            jax.ShapeDtypeStruct((feats, hid), BF16),
        ),
        in_specs=[in_vmem] * 2,
        out_specs=(in_hbm, in_hbm),
        scratch_shapes=[pltpu.SemaphoreType.DMA((5,))],
        compiler_params=pltpu.CompilerParams(vmem_limit_bytes=2 * 2**20),
        cost_estimate=pl.CostEstimate(flops=0, bytes_accessed=2 * feats * hid, transcendentals=0),
    )(input_grad.reshape(tb, feats), weight_grad)


def solution(mesh):
    in_specs = (P("col", "row"), P("row", "col"), P("row", "col"))
    out_specs = (P("col", "row"), P("row", "col"))
    return jax.shard_map(
        per_device, mesh=mesh, in_specs=in_specs, out_specs=out_specs, check_vma=False
    )
```

time: 134 us -> 132 us (0.985)
  the two profiles are of different devices: /device:TPU:0 before, /device:TPU:2 now
where the time goes in v2:
time: 132 us; the launch traced here: 130 us
  Pallas kernels  130 us (98%)
    pallas_call x1, Pallas kernels, per_device(): pl.pallas_call(kernel, out_shape=(vmem(1, 2, hb, feats), vmem(feats, hid)...  126 us
    pallas_call x1, Pallas kernels, per_device(): pl.pallas_call(write_out, out_shape=(jax.ShapeDtypeStruct((tb, feats), BF...  3.78 us

profile of v2, /device:TPU:2, one launch (start us, length us, event | category | flops | bytes accessed | tf_op | source)
XLA Modules:
  0.0 130.3 jit_solution(1062779915155370342)
XLA Ops:
  0.6 125.8 %shard_map.50 = (bf16[1,2,32,1536]{3,2,1,0:T(8,128)(2,1)S(1)}, bf16[1536,3072]{1,0:T(8,128)(2,1)S(1)}) custom-call(bf16[64,1536]{1,0:T(8,128)(2,1)} %acts_ref.1, bf16[1536,3072]{1,0:T(8,128)(2,1)} %w_ref.1, bf16[128,3072]{1,0:T(8,128)(2,1)} %og_ref.1), custom_call_target="tpu_custom_call" | custom-call | flops 28991029248 | bytes 18874368 | tf_op jit(solution)/shard_map/pallas_call | solution.py:483
  126.5 3.8 %shard_map.51 = (bf16[64,1536]{1,0:T(8,128)(2,1)}, bf16[1536,3072]{1,0:T(8,128)(2,1)}) custom-call(bf16[64,1536]{1,0:T(8,128)(2,1)S(1)} %bitcast.1, bf16[1536,3072]{1,0:T(8,128)(2,1)S(1)} %get-tuple-element.5.wg_ref), custom_call_target="tpu_custom_call" | custom-call | bytes 9437184 | tf_op jit(solution)/shard_map/pallas_call | solution.py:515

commit v3 on v2

--- a/solution.py
+++ b/solution.py
@@ -24,16 +24,16 @@
 
 def kernel(
     acts_ref, w_ref, og_ref, ig_ref, wg_ref,
-    acts, w, og, acts_t, part, sib_in, z_in_m, z_in_p, hidden, ig, y_in_m, y_in_p, xs, x_in,
+    acts, w_t, og, acts_t, part, sib_in, z_in_m, z_in_p, hidden, ig, y_in_m, y_in_p, xs, x_in,
     local_sem, send_sem, recv_sem,
 ):
     tb, feats = acts_ref.shape
     ob, hid = og_ref.shape
     half, quarter = ob // 2, ob // 4
     grp = 4 * tb
-    tn = tile_of(hid // 2, 512)
-    tf = tile_of(feats, 512)
-    tm = tile_of(feats, 256)
+    tv, tn, t3 = tile_of(hid // 2, 512), tile_of(hid // 2, 768), tile_of(hid, 1536)
+    tf, tm = tile_of(feats, 768), tile_of(feats, 256)
+    w = wg_ref
 
     row, col = lax.axis_index("row"), lax.axis_index("col")
     z, k = lax.div(row, 2), lax.rem(row, 2)
@@ -68,10 +68,14 @@
         pl.semaphore_signal(barrier, inc=1, device_id=to, device_id_type=MESH)
     own_acts = at(acts, (x * 4 + y) * tb, tb)
     load_acts = pltpu.make_async_copy(acts_ref, own_acts, local_sem.at[0])
-    load_w = pltpu.make_async_copy(w_ref, w, local_sem.at[1])
-    load_og = pltpu.make_async_copy(og_ref, og, local_sem.at[2])
+    load_og = pltpu.make_async_copy(og_ref, og, local_sem.at[1])
+    load_w = [
+        pltpu.make_async_copy(w_ref.at[pl.ds(m * tm, tm)], w.at[pl.ds(m * tm, tm)], local_sem.at[2 + m])
+        for m in range(feats // tm)
+    ]
     load_acts.start()
-    load_w.start()
+    for load in load_w:
+        load.start()
     load_og.start()
     load_acts.wait()
     pl.semaphore_wait(barrier, 7)
@@ -99,7 +103,22 @@
         for copy in copies:
             copy.wait_recv()
 
-    ag_finish(ag_forward(ag_start(lambda by: (nxt(x, by) * 4 + y) * tb, xp, xm)))
+    def turn_w(m, loaded=False):
+        if not loaded:
+            load_w[m].wait()
+
+        def tile(n, carry):
+            cols = pl.ds(pl.multiple_of(n * tm, tm), tm)
+            w_t[cols, m * tm:(m + 1) * tm] = w[m * tm:(m + 1) * tm, cols].T
+            return carry
+
+        lax.fori_loop(0, hid // tm, tile, 0)
+
+    g = ag_start(lambda by: (nxt(x, by) * 4 + y) * tb, xp, xm)
+    turn_w(0)
+    g = ag_forward(g)
+    turn_w(1)
+    ag_finish(g)
     order = [nxt(z, 2), nxt(z, 1), nxt(z, 3), z]
     y_gather = lambda s: ag_start(lambda by: (order[s] * 4 + nxt(y, by)) * tb, yp, ym)
 
@@ -130,13 +149,13 @@
         step = min(rows, 32)
         for r in range(0, rows, step):
             def tile(n, carry):
-                cols = pl.ds(pl.multiple_of(n * tn, tn), tn)
+                cols = pl.ds(pl.multiple_of(n * tv, tv), tv)
                 into = pl.ds(pl.multiple_of(dst_row + r, step), step)
                 total = dst[into, cols].astype(F32) + src[src_row + r:src_row + r + step, cols].astype(F32)
                 dst[into, cols] = total.astype(BF16)
                 return carry
 
-            lax.fori_loop(lo // tn, hi // tn, tile, 0)
+            lax.fori_loop(lo // tv, hi // tv, tile, 0)
 
     def core_sum(s, copy, lo=0, hi=hid):
         copy.wait_recv()
@@ -144,9 +163,13 @@
 
     mine = lambda s, start, size: part.at[s, pl.ds(pl.multiple_of(own_row + start, size), size)]
 
-    g = ag_forward(y_gather(0))
+    g = y_gather(0)
+    turn_w(2)
+    g = ag_forward(g)
     nx = y_gather(1)
-    load_w.wait()
+    turn_w(3)
+    for load in load_w[4:]:
+        load.wait()
     ag_finish(g)
     opp_p, opp_m = [], []
     for lo, hi in ((0, hid // 2), (hid // 2, hid)):
@@ -195,6 +218,8 @@
         return carry
 
     lax.fori_loop(0, feats // tm, turn, 0)
+    for m in range(4, feats // tm):
+        turn_w(m, True)
 
     dir_p.wait_recv()
     dir_m.wait_recv()
@@ -204,14 +229,14 @@
         start = q * quarter
 
         def tile(n, carry):
-            cols = pl.ds(pl.multiple_of(n * tn, tn), tn)
+            cols = pl.ds(pl.multiple_of(n * tv, tv), tv)
             own = part[3, pl.ds(pl.multiple_of(own_row + start, quarter), quarter), cols]
             pre = own.astype(F32) + from_m[:, cols].astype(F32) + from_p[:, cols].astype(F32)
             grad = og[start:start + quarter, cols].astype(F32) * gelu_slope(pre)
             hidden[z, 2 * k + q // 2, q % 2, :, cols] = grad.astype(BF16)
             return carry
 
-        lax.fori_loop(0, hid // tn, tile, 0)
+        lax.fori_loop(0, hid // tv, tile, 0)
         here = piece(z, k, q)
         return send(here, here, sib), send(here, here, zp), send(here, here, zm)
 
@@ -231,9 +256,7 @@
             cols = pl.ds(pl.multiple_of(n * tf, tf), tf)
             rows = [hidden[g, :, j].reshape(4 * hb, hid) for _, g, js in units for j in js]
             rows = rows[0] if len(rows) == 1 else jnp.concatenate(rows, axis=0)
-            share = lax.dot_general(
-                rows, w[cols, :], (((1,), (1,)), ((), ())), preferred_element_type=F32
-            ).astype(BF16)
+            share = jnp.dot(rows, w_t[:, cols], preferred_element_type=F32).astype(BF16)
             at_row = 0
             for s, _, js in units:
                 for j in js:
@@ -245,7 +268,7 @@
 
     def sum_into(out, terms):
         def tile(n, carry):
-            cols = pl.ds(pl.multiple_of(n * tf, tf), tf)
+            cols = pl.ds(pl.multiple_of(n * tv, tv), tv)
             for p in range(out.shape[0]):
                 for q in range(out.shape[1]):
                     total = terms[0][p, q, :, cols].astype(F32)
@@ -254,7 +277,7 @@
                     out[p, q, :, cols] = total.astype(BF16)
             return carry
 
-        lax.fori_loop(0, feats // tf, tile, 0)
+        lax.fori_loop(0, feats // tv, tile, 0)
 
     ha, hz = pl.ds(0, hb // 2), pl.ds(hb // 2, hb // 2)
 
@@ -292,7 +315,7 @@
         slot = lambda n: x_in.at[n, one, js]
         make = lambda rows, n, to: ready(mine_x(rows), slot(n), to)
         copies = (
-            make(ha, 0, xp), make(hz, 1, xm), make(hz, 2, xp), make(ha, 3, xp), make(ha, 4, xm), make(hz, 5, xm)
+            make(ha, 0, xp), make(hz, 0, xm), make(hz, 0, xp), make(ha, 1, xp), make(ha, 2, xm), make(hz, 3, xm)
         )
         return nxt(x, 4 - g), mine_x, slot, copies, (j0, nj)
 
@@ -327,7 +350,7 @@
         @pl.when(away == 1)
         def _():
             copies[1].wait_recv()
-            sum_into(mine_x(hz), [mine_x(hz), slot(1)])
+            sum_into(mine_x(hz), [mine_x(hz), slot(0)])
             copies[5].start()
 
     def x_finish(state):
@@ -338,8 +361,8 @@
         def _():
             for n in (2, 3, 4, 5):
                 copies[n].wait_recv()
-            sum_into(result(ha), [mine_x(ha), slot(3), slot(4)])
-            sum_into(result(hz), [mine_x(hz), slot(2), slot(5)])
+            sum_into(result(ha), [mine_x(ha), slot(1), slot(2)])
+            sum_into(result(hz), [mine_x(hz), slot(0), slot(3)])
 
         for role, used in ((2, (0, 1)), (3, (2, 3)), (1, (4, 5))):
             @pl.when(away == role)
@@ -352,15 +375,15 @@
         span = 8 * hb * 2
 
         def tile(n, carry):
-            cols = pl.ds(pl.multiple_of(n * tn, tn), tn)
-            units = jnp.concatenate([hidden[g, :, j, :, cols].reshape(4 * hb, tn) for g, j in rows_of], axis=0)
+            cols = pl.ds(pl.multiple_of(n * t3, t3), t3)
+            units = jnp.concatenate([hidden[g, :, j, :, cols].reshape(4 * hb, t3) for g, j in rows_of], axis=0)
             total = jnp.dot(acts_t[rows, first:first + span], units, preferred_element_type=F32)
             if later:
                 total = total + wg_ref[rows, cols].astype(F32)
             wg_ref[rows, cols] = total.astype(BF16)
             return carry
 
-        lax.fori_loop(0, hid // tn, tile, 0)
+        lax.fori_loop(0, hid // t3, tile, 0)
 
     blocks = feats // tm
 
@@ -490,7 +513,7 @@
         out_specs=(in_vmem, in_vmem),
         scratch_shapes=[
             vmem(tokens, feats),
-            vmem(feats, hid),
+            vmem(hid, feats),
             vmem(ob, hid),
             vmem(feats, tokens),
             vmem(4, 2 * ob, hid),
@@ -502,13 +525,13 @@
             vmem(3, 4, 2, hb // 2, feats),
             vmem(3, 4, 2, hb // 2, feats),
             vmem(4, 2, hb, feats),
-            vmem(6, 4, 2, hb // 2, feats),
-            pltpu.SemaphoreType.DMA((3,)),
+            vmem(4, 4, 2, hb // 2, feats),
+            pltpu.SemaphoreType.DMA((8,)),
             pltpu.SemaphoreType.DMA((N_SEMS,)),
             pltpu.SemaphoreType.DMA((N_SEMS,)),
         ],
         compiler_params=pltpu.CompilerParams(
-            collective_id=0, has_side_effects=True, vmem_limit_bytes=44 * 2**20
+            collective_id=0, has_side_effects=True, vmem_limit_bytes=50 * 2**20
         ),
         cost_estimate=pl.CostEstimate(flops=flops, bytes_accessed=4 * feats * hid, transcendentals=2 * ob * hid),
     )(acts, up_weight, out_grad)

time: 132 us -> 124 us (0.939)
  Pallas kernels: 130 us -> 120 us
    pallas_call x1, Pallas kernels: 126 us -> 117 us  [per_device(): pl.pallas_call(kernel, out_shape=(vmem(1, 2, hb, feats), vmem(feats, hid)...]
where the time goes in v3:
time: 124 us; the launch traced here: 121 us
  Pallas kernels  120 us (97%)
    pallas_call x1, Pallas kernels, per_device(): pl.pallas_call(kernel, out_shape=(vmem(1, 2, hb, feats), vmem(feats, hid)...  117 us
    pallas_call x1, Pallas kernels, per_device(): pl.pallas_call(write_out, out_shape=(jax.ShapeDtypeStruct((tb, feats), BF...  3.78 us

profile of v3, /device:TPU:2, one launch (start us, length us, event | category | flops | bytes accessed | tf_op | source)
XLA Modules:
  0.0 121.1 jit_solution(10015273170604046608)
XLA Ops:
  0.6 116.6 %shard_map.50 = (bf16[1,2,32,1536]{3,2,1,0:T(8,128)(2,1)S(1)}, bf16[1536,3072]{1,0:T(8,128)(2,1)S(1)}) custom-call(bf16[64,1536]{1,0:T(8,128)(2,1)} %acts_ref.1, bf16[1536,3072]{1,0:T(8,128)(2,1)} %w_ref.1, bf16[128,3072]{1,0:T(8,128)(2,1)} %og_ref.1), custom_call_target="tpu_custom_call" | custom-call | flops 28991029248 | bytes 18874368 | tf_op jit(solution)/shard_map/pallas_call | solution.py:506
  117.2 3.8 %shard_map.51 = (bf16[64,1536]{1,0:T(8,128)(2,1)}, bf16[1536,3072]{1,0:T(8,128)(2,1)}) custom-call(bf16[64,1536]{1,0:T(8,128)(2,1)S(1)} %bitcast.1, bf16[1536,3072]{1,0:T(8,128)(2,1)S(1)} %get-tuple-element.5.wg_ref), custom_call_target="tpu_custom_call" | custom-call | bytes 9437184 | tf_op jit(solution)/shard_map/pallas_call | solution.py:538

commit v4 on v3

--- a/solution.py
+++ b/solution.py
@@ -9,7 +9,7 @@
 
 F32, BF16 = jnp.float32, jnp.bfloat16
 MESH = pl.DeviceIdType.MESH
-N_SEMS = 144
+N_SEMS = 160
 
 
 def gelu_slope(pre):
@@ -29,8 +29,7 @@
 ):
     tb, feats = acts_ref.shape
     ob, hid = og_ref.shape
-    half, quarter = ob // 2, ob // 4
-    grp = 4 * tb
+    quarter = ob // 4
     tv, tn, t3 = tile_of(hid // 2, 512), tile_of(hid // 2, 768), tile_of(hid, 1536)
     tf, tm = tile_of(feats, 768), tile_of(feats, 256)
     w = wg_ref
@@ -60,31 +59,36 @@
         sent[-1] = copy
         return copy
 
-    def at(ref, start, size):
-        return ref.at[pl.ds(pl.multiple_of(start, size), size)]
+    hb = tb // 2
+
+    def step_of(group):
+        away = nxt(group, 4 - z)
+        odd, far = lax.rem(away, 2), lax.div(away, 2)
+        return odd * (2 - lax.rem(far + y, 2)) + (1 - odd) * (3 - 3 * far)
 
     barrier = pltpu.get_barrier_semaphore()
     for to in (sib, zp, zm, xp, xm, yp, ym):
         pl.semaphore_signal(barrier, inc=1, device_id=to, device_id_type=MESH)
-    own_acts = at(acts, (x * 4 + y) * tb, tb)
-    load_acts = pltpu.make_async_copy(acts_ref, own_acts, local_sem.at[0])
-    load_og = pltpu.make_async_copy(og_ref, og, local_sem.at[1])
+    load_acts = [
+        pltpu.make_async_copy(acts_ref.at[pl.ds(j * hb, hb)], acts.at[step_of(x), y, j], local_sem.at[j])
+        for j in range(2)
+    ]
+    load_og = pltpu.make_async_copy(og_ref, og, local_sem.at[2])
     load_w = [
-        pltpu.make_async_copy(w_ref.at[pl.ds(m * tm, tm)], w.at[pl.ds(m * tm, tm)], local_sem.at[2 + m])
+        pltpu.make_async_copy(w_ref.at[pl.ds(m * tm, tm)], w.at[pl.ds(m * tm, tm)], local_sem.at[3 + m])
         for m in range(feats // tm)
     ]
-    load_acts.start()
-    for load in load_w:
+    for load in (*load_acts, *load_w, load_og):
         load.start()
-    load_og.start()
-    load_acts.wait()
+    for load in load_acts:
+        load.wait()
     pl.semaphore_wait(barrier, 7)
 
-    hb = tb // 2
+    low16, high16 = pl.ds(0, hb // 2), pl.ds(hb // 2, hb // 2)
 
     def ag_start(block, to_p, to_m):
-        a = lambda by: at(acts, block(by), hb)
-        b = lambda by: at(acts, block(by) + hb, hb)
+        a = lambda by: block(by, low16)
+        b = lambda by: block(by, high16)
         pa = send(a(0), a(0), to_p)
         mb = send(b(0), b(0), to_m)
         pb = send(b(0), b(0), to_p)
@@ -103,6 +107,12 @@
         for copy in copies:
             copy.wait_recv()
 
+    def x_gather(j):
+        return ag_start(lambda by, rows: acts.at[step_of(nxt(x, by)), y, j, rows], xp, xm)
+
+    def y_gather(s, j0, nj):
+        return ag_start(lambda by, rows: acts.at[s, nxt(y, by), pl.ds(j0, nj), rows], yp, ym)
+
     def turn_w(m, loaded=False):
         if not loaded:
             load_w[m].wait()
@@ -114,106 +124,109 @@
 
         lax.fori_loop(0, hid // tm, tile, 0)
 
-    g = ag_start(lambda by: (nxt(x, by) * 4 + y) * tb, xp, xm)
-    turn_w(0)
-    g = ag_forward(g)
-    turn_w(1)
-    ag_finish(g)
-    order = [nxt(z, 2), nxt(z, 1), nxt(z, 3), z]
-    y_gather = lambda s: ag_start(lambda by: (order[s] * 4 + nxt(y, by)) * tb, yp, ym)
-
-    def dot1(s, lo=0, hi=hid):
-        rows = pl.ds(pl.multiple_of(order[s] * grp, grp), grp)
-        theirs = part.at[s, pl.ds(pl.multiple_of((1 - k) * ob, ob), ob)]
+    def dot1(s, j0, nj):
+        js = pl.ds(j0, nj)
         sem = len(sent)
 
         def to_sib(cols):
             return pltpu.make_async_remote_copy(
-                src_ref=theirs.at[:, cols], dst_ref=sib_in.at[s, :, cols], send_sem=send_sem.at[sem],
-                recv_sem=recv_sem.at[sem], device_id=sib, device_id_type=MESH,
+                src_ref=part.at[s, pl.ds(2 * (1 - k), 2), js, :, cols], dst_ref=sib_in.at[s, :, js, :, cols],
+                send_sem=send_sem.at[sem], recv_sem=recv_sem.at[sem], device_id=sib, device_id_type=MESH,
             )
 
         def tile(n, carry):
             cols = pl.ds(pl.multiple_of(n * tn, tn), tn)
-            part[s, :, cols] = jnp.dot(acts[rows, :], w[:, cols], preferred_element_type=F32).astype(BF16)
+            share = jnp.dot(
+                acts[s, :, js].reshape(4 * nj * hb, feats), w[:, cols], preferred_element_type=F32
+            )
+            part[s, :, js, :, cols] = share.astype(BF16).reshape(4, nj, hb, tn)
             to_sib(cols).start()
             return carry
 
-        lax.fori_loop(lo // tn, hi // tn, tile, 0)
-        sent.append(to_sib(pl.ds(lo, hi - lo)))
+        lax.fori_loop(0, hid // tn, tile, 0)
+        sent.append(to_sib(pl.ds(0, hid)))
         return sent[-1]
 
-    own_row = pl.multiple_of(k * ob, ob)
-
-    def add_into(dst, dst_row, src, src_row, rows, lo=0, hi=hid):
-        step = min(rows, 32)
-        for r in range(0, rows, step):
-            def tile(n, carry):
-                cols = pl.ds(pl.multiple_of(n * tv, tv), tv)
-                into = pl.ds(pl.multiple_of(dst_row + r, step), step)
-                total = dst[into, cols].astype(F32) + src[src_row + r:src_row + r + step, cols].astype(F32)
-                dst[into, cols] = total.astype(BF16)
-                return carry
-
-            lax.fori_loop(lo // tv, hi // tv, tile, 0)
-
-    def core_sum(s, copy, lo=0, hi=hid):
+    def add_into(dst, src):
+        def tile(n, carry):
+            cols = pl.ds(pl.multiple_of(n * tv, tv), tv)
+            for j in range(dst.shape[0]):
+                total = dst[j, :, cols].astype(F32) + src[j, :, cols].astype(F32)
+                dst[j, :, cols] = total.astype(BF16)
+            return carry
+
+        lax.fori_loop(0, hid // tv, tile, 0)
+
+    def core_sum(s, copy, j0, nj):
         copy.wait_recv()
-        add_into(part.at[s], own_row, sib_in.at[s], 0, ob, lo, hi)
-
-    mine = lambda s, start, size: part.at[s, pl.ds(pl.multiple_of(own_row + start, size), size)]
-
-    g = y_gather(0)
-    turn_w(2)
-    g = ag_forward(g)
-    nx = y_gather(1)
-    turn_w(3)
-    for load in load_w[4:]:
+        js = pl.ds(j0, nj)
+        for way in range(2):
+            add_into(part.at[s, 2 * k + way, js], sib_in.at[s, way, js])
+
+    mine = lambda s, way: part.at[s, 2 * k + way]
+    gx = x_gather(0)
+    turn_w(0)
+    gx0 = ag_forward(gx)
+    gx = x_gather(1)
+    ag_finish(gx0)
+    g = y_gather(0, 0, 1)
+    turn_w(1)
+    gx1 = ag_forward(gx)
+    g0 = ag_forward(g)
+    ag_finish(gx1)
+    g = y_gather(0, 1, 1)
+    for load in load_w[2:]:
         load.wait()
-    ag_finish(g)
+    ag_finish(g0)
     opp_p, opp_m = [], []
-    for lo, hi in ((0, hid // 2), (hid // 2, hid)):
-        c = dot1(0, lo, hi)
-        if lo == 0:
-            g = ag_forward(nx)
-            nx = y_gather(2)
-        core_sum(0, c, lo, hi)
-        cols = pl.ds(lo, hi - lo)
-        opp_p.append(send(mine(0, 0, half).at[:, cols], z_in_m.at[0, :, cols], zp))
-        opp_m.append(send(mine(0, half, half).at[:, cols], z_in_p.at[0, :, cols], zm))
-    ag_finish(g)
-    c = dot1(1)
-    g = ag_forward(nx)
-    nx = y_gather(3)
-    core_sum(1, c)
-    dir_p = send(mine(1, half, half), z_in_m.at[1], zp)
-    ag_finish(g)
-    c = dot1(2)
-    g = ag_forward(nx)
-    core_sum(2, c)
-    dir_m = send(mine(2, 0, half), z_in_p.at[1], zm)
-    ag_finish(g)
-    c = dot1(3)
-    for copy in opp_p:
-        copy.wait_recv()
-    add_into(part.at[1], own_row, z_in_m.at[0], 0, half)
-    acc_p = [send(mine(1, j * quarter, quarter), z_in_m.at[2, pl.ds(j * quarter, quarter)], zp) for j in range(2)]
-    for copy in opp_m:
-        copy.wait_recv()
-    add_into(part.at[2], own_row + half, z_in_p.at[0], 0, half)
-    acc_m = [send(mine(2, half + j * quarter, quarter), z_in_p.at[2, pl.ds(j * quarter, quarter)], zm) for j in range(2)]
-    core_sum(3, c)
+    c = dot1(0, 0, 1)
+    g0 = ag_forward(g)
+    g = y_gather(1, 0, 2)
+    core_sum(0, c, 0, 1)
+    opp_p.append(send(mine(0, 0).at[0], z_in_m.at[0, 0], zp))
+    opp_m.append(send(mine(0, 1).at[0], z_in_p.at[0, 0], zm))
+    ag_finish(g0)
+    c = dot1(0, 1, 1)
+    g0 = ag_forward(g)
+    g = y_gather(2, 0, 2)
+    core_sum(0, c, 1, 1)
+    opp_p.append(send(mine(0, 0).at[1], z_in_m.at[0, 1], zp))
+    opp_m.append(send(mine(0, 1).at[1], z_in_p.at[0, 1], zm))
+    turn_w(2, True)
+    ag_finish(g0)
+    c = dot1(1, 0, 2)
+    g0 = ag_forward(g)
+    g = y_gather(3, 0, 2)
+    core_sum(1, c, 0, 2)
+    dir_p = send(mine(1, 1), z_in_m.at[1], zp)
+    dir_m = send(mine(1, 0), z_in_p.at[1], zm)
+    turn_w(3, True)
+    ag_finish(g0)
+    c = dot1(2, 0, 2)
+    g0 = ag_forward(g)
+    core_sum(2, c, 0, 2)
+    acc_p, acc_m = [], []
+    for j in range(2):
+        one = pl.ds(j, 1)
+        opp_p[j].wait_recv()
+        add_into(mine(2, 0).at[one], z_in_m.at[0, one])
+        acc_p.append(send(mine(2, 0).at[j], z_in_m.at[2, j], zp))
+        opp_m[j].wait_recv()
+        add_into(mine(2, 1).at[one], z_in_p.at[0, one])
+        acc_m.append(send(mine(2, 1).at[j], z_in_p.at[2, j], zm))
+    ag_finish(g0)
+    c = dot1(3, 0, 2)
+    core_sum(3, c, 0, 2)
     load_og.wait()
 
-    tokens_of = [
-        (z, 0), (z, 1), (nxt(z, 3), 0), (nxt(z, 1), 0),
-        (nxt(z, 3), 1), (nxt(z, 1), 1), (nxt(z, 2), 0), (nxt(z, 2), 1),
-    ]
+    low, high, opp = nxt(z, 3), nxt(z, 1), nxt(z, 2)
+    tokens_of = [(z, 0), (z, 1), (low, 0), (high, 0), (low, 1), (high, 1), (opp, 0), (opp, 1)]
+    held_in = [(3, 3), (3, 3), (1, 2), (2, 1), (1, 2), (2, 1), (0, 0), (0, 0)]
 
     def turn(n, carry):
         cols = pl.ds(pl.multiple_of(n * tm, tm), tm)
-        for t, (g, j) in enumerate(tokens_of):
-            rows = [at(acts, g * grp + b * tb + j * hb, hb)[:, cols] for b in range(4)]
+        for t, steps in enumerate(held_in):
+            rows = [acts[steps[b % 2], b, tokens_of[t][1], :, cols] for b in range(4)]
             acts_t[cols, t * 4 * hb:(t + 1) * 4 * hb] = jnp.concatenate(rows, axis=0).T
         return carry
 
@@ -230,7 +243,7 @@
 
         def tile(n, carry):
             cols = pl.ds(pl.multiple_of(n * tv, tv), tv)
-            own = part[3, pl.ds(pl.multiple_of(own_row + start, quarter), quarter), cols]
+            own = part[3, 2 * k + q // 2, q % 2, :, cols]
             pre = own.astype(F32) + from_m[:, cols].astype(F32) + from_p[:, cols].astype(F32)
             grad = og[start:start + quarter, cols].astype(F32) * gelu_slope(pre)
             hidden[z, 2 * k + q // 2, q % 2, :, cols] = grad.astype(BF16)
@@ -243,13 +256,10 @@
     arrivals = (0, 2, 1, 3)
     own_sends = {}
     for j in range(2):
-        rows = pl.ds(j * quarter, quarter)
         acc_p[j].wait_recv()
-        own_sends[j] = slope_piece(j, z_in_m.at[2, rows], z_in_p.at[1, rows])
+        own_sends[j] = slope_piece(j, z_in_m.at[2, j], z_in_p.at[1, j])
         acc_m[j].wait_recv()
-        own_sends[2 + j] = slope_piece(2 + j, z_in_m.at[1, rows], z_in_p.at[2, rows])
-
-    low, high, opp = nxt(z, 3), nxt(z, 1), nxt(z, 2)
+        own_sends[2 + j] = slope_piece(2 + j, z_in_m.at[1, j], z_in_p.at[2, j])
 
     def dot2(units):
         def tile(n, carry):
@@ -495,7 +505,7 @@
     tb, feats = acts.shape
     ob, hid = out_grad.shape
     tokens = 16 * tb
-    hb, half = tb // 2, ob // 2
+    hb = tb // 2
     vmem = lambda *shape: pltpu.VMEM(shape, BF16)
     in_hbm = pl.BlockSpec(memory_space=pltpu.HBM)
     in_vmem = pl.BlockSpec(memory_space=pltpu.VMEM)
@@ -512,21 +522,21 @@
         in_specs=[in_hbm] * 3,
         out_specs=(in_vmem, in_vmem),
         scratch_shapes=[
-            vmem(tokens, feats),
+            vmem(4, 4, 2, hb, feats),
             vmem(hid, feats),
             vmem(ob, hid),
             vmem(feats, tokens),
-            vmem(4, 2 * ob, hid),
-            vmem(4, ob, hid),
-            vmem(3, half, hid),
-            vmem(3, half, hid),
+            vmem(4, 4, 2, hb, hid),
+            vmem(4, 2, 2, hb, hid),
+            vmem(3, 2, hb, hid),
+            vmem(3, 2, hb, hid),
             vmem(4, 4, 2, hb, hid),
             vmem(4, 2, 4, hb, feats),
             vmem(3, 4, 2, hb // 2, feats),
             vmem(3, 4, 2, hb // 2, feats),
             vmem(4, 2, hb, feats),
             vmem(4, 4, 2, hb // 2, feats),
-            pltpu.SemaphoreType.DMA((8,)),
+            pltpu.SemaphoreType.DMA((9,)),
             pltpu.SemaphoreType.DMA((N_SEMS,)),
             pltpu.SemaphoreType.DMA((N_SEMS,)),
         ],

time: 124 us -> 119 us (0.960); the launches traced: 121 us -> 119 us
    pallas_call x1, Pallas kernels: 117 us -> 115 us  [per_device(): pl.pallas_call(kernel, out_shape=(vmem(1, 2, hb, feats), vmem(feats, hid)...]
where the time goes in v4:
time: 119 us
  Pallas kernels  119 us (100%)
    pallas_call x1, Pallas kernels, per_device(): pl.pallas_call(kernel, out_shape=(vmem(1, 2, hb, feats), vmem(feats, hid)...  115 us
    pallas_call x1, Pallas kernels, per_device(): pl.pallas_call(write_out, out_shape=(jax.ShapeDtypeStruct((tb, feats), BF...  3.78 us

profile of v4, /device:TPU:2, one launch (start us, length us, event | category | flops | bytes accessed | tf_op | source)
XLA Modules:
  0.0 119.4 jit_solution(18377210789142876796)
XLA Ops:
  0.6 114.8 %shard_map.50 = (bf16[1,2,32,1536]{3,2,1,0:T(8,128)(2,1)S(1)}, bf16[1536,3072]{1,0:T(8,128)(2,1)S(1)}) custom-call(bf16[64,1536]{1,0:T(8,128)(2,1)} %acts_ref.1, bf16[1536,3072]{1,0:T(8,128)(2,1)} %w_ref.1, bf16[128,3072]{1,0:T(8,128)(2,1)} %og_ref.1), custom_call_target="tpu_custom_call" | custom-call | flops 28991029248 | bytes 18874368 | tf_op jit(solution)/shard_map/pallas_call | solution.py:516
  115.4 3.8 %shard_map.51 = (bf16[64,1536]{1,0:T(8,128)(2,1)}, bf16[1536,3072]{1,0:T(8,128)(2,1)}) custom-call(bf16[64,1536]{1,0:T(8,128)(2,1)S(1)} %bitcast.1, bf16[1536,3072]{1,0:T(8,128)(2,1)S(1)} %get-tuple-element.5.wg_ref), custom_call_target="tpu_custom_call" | custom-call | bytes 9437184 | tf_op jit(solution)/shard_map/pallas_call | solution.py:548

commit v5 on v4

--- a/solution.py
+++ b/solution.py
@@ -30,7 +30,7 @@
     tb, feats = acts_ref.shape
     ob, hid = og_ref.shape
     quarter = ob // 4
-    tv, tn, t3 = tile_of(hid // 2, 512), tile_of(hid // 2, 768), tile_of(hid, 1536)
+    tv, tn, t3 = tile_of(hid // 2, 512), tile_of(hid // 2, 768), tile_of(hid, 256)
     tf, tm = tile_of(feats, 768), tile_of(feats, 256)
     w = wg_ref
 
@@ -168,14 +168,16 @@
     turn_w(0)
     gx0 = ag_forward(gx)
     gx = x_gather(1)
+    turn_w(1)
     ag_finish(gx0)
     g = y_gather(0, 0, 1)
-    turn_w(1)
+    turn_w(2)
     gx1 = ag_forward(gx)
     g0 = ag_forward(g)
+    turn_w(3)
     ag_finish(gx1)
     g = y_gather(0, 1, 1)
-    for load in load_w[2:]:
+    for load in load_w[4:]:
         load.wait()
     ag_finish(g0)
     opp_p, opp_m = [], []
@@ -192,7 +194,6 @@
     core_sum(0, c, 1, 1)
     opp_p.append(send(mine(0, 0).at[1], z_in_m.at[0, 1], zp))
     opp_m.append(send(mine(0, 1).at[1], z_in_p.at[0, 1], zm))
-    turn_w(2, True)
     ag_finish(g0)
     c = dot1(1, 0, 2)
     g0 = ag_forward(g)
@@ -200,7 +201,6 @@
     core_sum(1, c, 0, 2)
     dir_p = send(mine(1, 1), z_in_m.at[1], zp)
     dir_m = send(mine(1, 0), z_in_p.at[1], zm)
-    turn_w(3, True)
     ag_finish(g0)
     c = dot1(2, 0, 2)
     g0 = ag_forward(g)
@@ -380,30 +380,27 @@
                 for n in used:
                     copies[n].wait_send()
 
-    def dot3(m, rows_of, first, later):
-        rows = pl.ds(m * tm, tm)
-        span = 8 * hb * 2
+    def dot3(lo, hi, rows_of, first, later):
+        span = 16 * hb
 
         def tile(n, carry):
             cols = pl.ds(pl.multiple_of(n * t3, t3), t3)
             units = jnp.concatenate([hidden[g, :, j, :, cols].reshape(4 * hb, t3) for g, j in rows_of], axis=0)
-            total = jnp.dot(acts_t[rows, first:first + span], units, preferred_element_type=F32)
+            total = jnp.dot(acts_t[:, first:first + span], units, preferred_element_type=F32)
             if later:
-                total = total + wg_ref[rows, cols].astype(F32)
-            wg_ref[rows, cols] = total.astype(BF16)
-            return carry
-
-        lax.fori_loop(0, hid // t3, tile, 0)
-
-    blocks = feats // tm
+                total = total + wg_ref[:, cols].astype(F32)
+            wg_ref[:, cols] = total.astype(BF16)
+            return carry
+
+        lax.fori_loop(lo, hi, tile, 0)
+
+    blocks = hid // t3
 
     def early(lo, hi):
-        for m in range(lo, hi):
-            dot3(m, tokens_of[:4], 0, False)
+        dot3(lo * blocks // 6, hi * blocks // 6, tokens_of[:4], 0, False)
 
     def late(lo, hi):
-        for m in range(lo, hi):
-            dot3(m, tokens_of[4:], 8 * hb * 2, True)
+        dot3(lo * blocks // 6, hi * blocks // 6, tokens_of[4:], 16 * hb, True)
 
     def neighbours(qs):
         copies = []
@@ -446,7 +443,7 @@
     early(0, 2)
     y1 = y_middle(y1)
     x_middle(x0)
-    early(2, blocks)
+    early(2, 6)
     y_finish(y1)
     from_sib = neighbours((1, 3))
     x_finish(x0)
@@ -481,7 +478,7 @@
     x_finish(x1)
     x_finish(x2)
     x_finish(x3)
-    late(3, blocks)
+    late(3, 6)
     x_finish(x4)
 
     for copy in sent:

time: 119 us -> 118 us (level)
  Pallas kernels: 119 us -> 117 us
    pallas_call x1, Pallas kernels: 115 us -> 114 us  [per_device(): pl.pallas_call(kernel, out_shape=(vmem(1, 2, hb, feats), vmem(feats, hid)...]
where the time goes in v5:
time: 118 us
  Pallas kernels  117 us (99%)
    pallas_call x1, Pallas kernels, per_device(): pl.pallas_call(kernel, out_shape=(vmem(1, 2, hb, feats), vmem(feats, hid)...  114 us
    pallas_call x1, Pallas kernels, per_device(): pl.pallas_call(write_out, out_shape=(jax.ShapeDtypeStruct((tb, feats), BF...  3.78 us

profile of v5, /device:TPU:2, one launch (start us, length us, event | category | flops | bytes accessed | tf_op | source)
XLA Modules:
  0.0 118.0 jit_solution(14728237651267415073)
XLA Ops:
  0.6 113.6 %shard_map.50 = (bf16[1,2,32,1536]{3,2,1,0:T(8,128)(2,1)S(1)}, bf16[1536,3072]{1,0:T(8,128)(2,1)S(1)}) custom-call(bf16[64,1536]{1,0:T(8,128)(2,1)} %acts_ref.1, bf16[1536,3072]{1,0:T(8,128)(2,1)} %w_ref.1, bf16[128,3072]{1,0:T(8,128)(2,1)} %og_ref.1), custom_call_target="tpu_custom_call" | custom-call | flops 28991029248 | bytes 18874368 | tf_op jit(solution)/shard_map/pallas_call | solution.py:513
  114.2 3.8 %shard_map.51 = (bf16[64,1536]{1,0:T(8,128)(2,1)}, bf16[1536,3072]{1,0:T(8,128)(2,1)}) custom-call(bf16[64,1536]{1,0:T(8,128)(2,1)S(1)} %bitcast.1, bf16[1536,3072]{1,0:T(8,128)(2,1)S(1)} %get-tuple-element.5.wg_ref), custom_call_target="tpu_custom_call" | custom-call | bytes 9437184 | tf_op jit(solution)/shard_map/pallas_call | solution.py:545

commit v6 on v5

--- a/solution.py
+++ b/solution.py
@@ -30,8 +30,8 @@
     tb, feats = acts_ref.shape
     ob, hid = og_ref.shape
     quarter = ob // 4
-    tv, tn, t3 = tile_of(hid // 2, 512), tile_of(hid // 2, 768), tile_of(hid, 256)
-    tf, tm = tile_of(feats, 768), tile_of(feats, 256)
+    tv, tn, t3 = tile_of(hid // 2, 512), tile_of(hid // 2, 1536), tile_of(hid, 512)
+    tf, tm = tile_of(feats, 1536), tile_of(feats, 256)
     w = wg_ref
 
     row, col = lax.axis_index("row"), lax.axis_index("col")
@@ -183,24 +183,26 @@
     opp_p, opp_m = [], []
     c = dot1(0, 0, 1)
     g0 = ag_forward(g)
-    g = y_gather(1, 0, 2)
+    g = y_gather(1, 0, 1)
     core_sum(0, c, 0, 1)
     opp_p.append(send(mine(0, 0).at[0], z_in_m.at[0, 0], zp))
     opp_m.append(send(mine(0, 1).at[0], z_in_p.at[0, 0], zm))
     ag_finish(g0)
     c = dot1(0, 1, 1)
     g0 = ag_forward(g)
-    g = y_gather(2, 0, 2)
+    g = y_gather(1, 1, 1)
     core_sum(0, c, 1, 1)
     opp_p.append(send(mine(0, 0).at[1], z_in_m.at[0, 1], zp))
     opp_m.append(send(mine(0, 1).at[1], z_in_p.at[0, 1], zm))
-    ag_finish(g0)
-    c = dot1(1, 0, 2)
-    g0 = ag_forward(g)
-    g = y_gather(3, 0, 2)
-    core_sum(1, c, 0, 2)
-    dir_p = send(mine(1, 1), z_in_m.at[1], zp)
-    dir_m = send(mine(1, 0), z_in_p.at[1], zm)
+    dir_p, dir_m = [], []
+    for j in range(2):
+        ag_finish(g0)
+        c = dot1(1, j, 1)
+        g0 = ag_forward(g)
+        g = y_gather(2 + j, 0, 2)
+        core_sum(1, c, j, 1)
+        dir_p.append(send(mine(1, 1).at[j], z_in_m.at[1, j], zp))
+        dir_m.append(send(mine(1, 0).at[j], z_in_p.at[1, j], zm))
     ag_finish(g0)
     c = dot1(2, 0, 2)
     g0 = ag_forward(g)
@@ -234,8 +236,8 @@
     for m in range(4, feats // tm):
         turn_w(m, True)
 
-    dir_p.wait_recv()
-    dir_m.wait_recv()
+    for copy in (*dir_p, *dir_m):
+        copy.wait_recv()
     piece = lambda zz, kk, q: hidden.at[zz, 2 * kk + q // 2, q % 2]
 
     def slope_piece(q, from_m, from_p):
@@ -443,13 +445,16 @@
     early(0, 2)
     y1 = y_middle(y1)
     x_middle(x0)
-    early(2, 6)
+    from_sib = neighbours((1,))
+    early(2, 4)
     y_finish(y1)
-    from_sib = neighbours((1, 3))
+    from_sib += neighbours((3,))
     x_finish(x0)
+    early(4, 5)
     arrived(from_sib)
     dot2([(1, low, (1,)), (2, high, (1,))])
     y2 = y_start(1, 2, 1, 1)
+    early(5, 6)
     from_sib = opposite((0, 2))
     y2 = y_middle(y2)
     arrived(from_sib)

time: 118 us -> 120 us (1.017)
  Pallas kernels: 117 us -> 119 us
    pallas_call x1, Pallas kernels: 114 us -> 115 us  [per_device(): pl.pallas_call(kernel, out_shape=(vmem(1, 2, hb, feats), vmem(feats, hid)...]
where the time goes in v6:
time: 120 us
  Pallas kernels  119 us (99%)
    pallas_call x1, Pallas kernels, per_device(): pl.pallas_call(kernel, out_shape=(vmem(1, 2, hb, feats), vmem(feats, hid)...  115 us
    pallas_call x1, Pallas kernels, per_device(): pl.pallas_call(write_out, out_shape=(jax.ShapeDtypeStruct((tb, feats), BF...  3.78 us

profile of v6, /device:TPU:2, one launch (start us, length us, event | category | flops | bytes accessed | tf_op | source)
XLA Modules:
  0.0 119.9 jit_solution(15339597619168360140)
XLA Ops:
  0.6 115.3 %shard_map.50 = (bf16[1,2,32,1536]{3,2,1,0:T(8,128)(2,1)S(1)}, bf16[1536,3072]{1,0:T(8,128)(2,1)S(1)}) custom-call(bf16[64,1536]{1,0:T(8,128)(2,1)} %acts_ref.1, bf16[1536,3072]{1,0:T(8,128)(2,1)} %w_ref.1, bf16[128,3072]{1,0:T(8,128)(2,1)} %og_ref.1), custom_call_target="tpu_custom_call" | custom-call | flops 28991029248 | bytes 18874368 | tf_op jit(solution)/shard_map/pallas_call | solution.py:518
  116.0 3.8 %shard_map.51 = (bf16[64,1536]{1,0:T(8,128)(2,1)}, bf16[1536,3072]{1,0:T(8,128)(2,1)}) custom-call(bf16[64,1536]{1,0:T(8,128)(2,1)S(1)} %bitcast.1, bf16[1536,3072]{1,0:T(8,128)(2,1)S(1)} %get-tuple-element.5.wg_ref), custom_call_target="tpu_custom_call" | custom-call | bytes 9437184 | tf_op jit(solution)/shard_map/pallas_call | solution.py:550

commit v7 on v0

v7 whole, which is shorter than its diff:
```python
import functools

import jax
import jax.numpy as jnp
from jax import lax
from jax.experimental import pallas as pl
from jax.experimental.pallas import tpu as pltpu
from jax.sharding import PartitionSpec as P

F32, BF16 = jnp.float32, jnp.bfloat16
MESH = pl.DeviceIdType.MESH
N_SEMS = 160


def gelu_slope(pre):
    cdf = 0.5 * (1.0 + lax.erf(pre * 0.7071067811865476))
    dens = jnp.exp(-0.5 * pre * pre) * 0.3989422804014327
    return cdf + pre * dens


def tile_of(size, want):
    return want if size % want == 0 else size


def kernel(
    acts_ref, w_ref, og_ref, ig_ref, wg_ref,
    acts, w_t, og, acts_t, part, sib_in, z_in, hidden, ig, y_in_m, y_in_p, xs, x_in,
    local_sem, send_sem, recv_sem,
):
    tb, feats = acts_ref.shape
    ob, hid = og_ref.shape
    quarter = ob // 4
    tv, tn, t3 = tile_of(hid // 2, 512), tile_of(hid // 2, 768), tile_of(hid, 256)
    tf, tm = tile_of(feats, 768), tile_of(feats, 256)
    w = wg_ref

    row, col = lax.axis_index("row"), lax.axis_index("col")
    z, k = lax.div(row, 2), lax.rem(row, 2)
    x, y = lax.div(col, 4), lax.rem(col, 4)
    nxt = lambda v, by: lax.rem(v + by, 4)
    sib = {"row": z * 2 + (1 - k)}
    zp, zm = {"row": nxt(z, 1) * 2 + k}, {"row": nxt(z, 3) * 2 + k}
    xp, xm = {"col": nxt(x, 1) * 4 + y}, {"col": nxt(x, 3) * 4 + y}
    yp, ym = {"col": x * 4 + nxt(y, 1)}, {"col": x * 4 + nxt(y, 3)}

    made = []

    def link(src, dst, to, always=True):
        i = len(made)
        copy = pltpu.make_async_remote_copy(
            src_ref=src, dst_ref=dst, send_sem=send_sem.at[i], recv_sem=recv_sem.at[i],
            device_id=to, device_id_type=MESH,
        )
        made.append(copy if always else None)
        return copy

    def at_turn(n, turn, *work):
        @pl.when(n == turn)
        def _():
            for do in work:
                do()

    def arrived(copies):
        for copy in copies:
            copy.wait_recv()

    hb = tb // 2

    def step_of(group):
        away = nxt(group, 4 - z)
        odd, far = lax.rem(away, 2), lax.div(away, 2)
        return odd * (2 - lax.rem(far + y, 2)) + (1 - odd) * (3 - 3 * far)

    barrier = pltpu.get_barrier_semaphore()
    for to in (sib, zp, zm, xp, xm, yp, ym):
        pl.semaphore_signal(barrier, inc=1, device_id=to, device_id_type=MESH)
    load_acts = [
        pltpu.make_async_copy(acts_ref.at[pl.ds(j * hb, hb)], acts.at[step_of(x), y, j], local_sem.at[j])
        for j in range(2)
    ]
    load_og = pltpu.make_async_copy(og_ref, og, local_sem.at[2])
    load_w = [
        pltpu.make_async_copy(w_ref.at[pl.ds(m * tm, tm)], w.at[pl.ds(m * tm, tm)], local_sem.at[3 + m])
        for m in range(feats // tm)
    ]
    for load in (*load_acts, *load_w, load_og):
        load.start()
    for load in load_acts:
        load.wait()
    pl.semaphore_wait(barrier, 7)

    ha, hz = pl.ds(0, hb // 2), pl.ds(hb // 2, hb // 2)

    class Gather:
        def __init__(self, block, to_p, to_m):
            a, b = (lambda by: block(by, ha)), (lambda by: block(by, hz))
            self.pa, self.mb = link(a(0), a(0), to_p), link(b(0), b(0), to_m)
            self.pb, self.ma = link(b(0), b(0), to_p), link(a(0), a(0), to_m)
            self.fa, self.fb = link(a(3), a(3), to_p), link(b(1), b(1), to_m)

        def start(self):
            for copy in (self.pa, self.mb, self.pb, self.ma):
                copy.start()

        def forward(self):
            self.pa.wait_recv()
            self.fa.start()
            self.mb.wait_recv()
            self.fb.start()

        def finish(self):
            arrived((self.pb, self.ma, self.fa, self.fb))

    def x_gather(j):
        return Gather(lambda by, rows: acts.at[step_of(nxt(x, by)), y, j, rows], xp, xm)

    def y_gather(s, j0, nj):
        return Gather(lambda by, rows: acts.at[s, nxt(y, by), pl.ds(j0, nj), rows], yp, ym)

    gx = [x_gather(0), x_gather(1)]
    gy = [y_gather(0, 0, 1), y_gather(0, 1, 1), y_gather(1, 0, 2), y_gather(2, 0, 2), y_gather(3, 0, 2)]

    def turn_w(m):
        to = pl.ds(pl.multiple_of(m * tm, tm), tm)

        def tile(n, carry):
            cols = pl.ds(pl.multiple_of(n * tm, tm), tm)
            w_t[cols, to] = w[to, cols].T
            return carry

        lax.fori_loop(0, hid // tm, tile, 0)

    theirs = lambda s, js, cols: part.at[s, pl.ds(2 * (1 - k), 2), js, :, cols]
    every = pl.ds(0, hid)
    sib_first = len(made)
    for s, j0, nj in ((0, 0, 1), (0, 1, 1), (1, 0, 2), (2, 0, 2), (3, 0, 2)):
        js = pl.ds(j0, nj)
        link(theirs(s, js, every), sib_in.at[s, :, js, :, every], sib)

    def add_into(dst, src):
        def tile(n, carry):
            cols = pl.ds(pl.multiple_of(n * tv, tv), tv)
            for j in range(dst.shape[0]):
                total = dst[j, :, cols].astype(F32) + src[j, :, cols].astype(F32)
                dst[j, :, cols] = total.astype(BF16)
            return carry

        lax.fori_loop(0, hid // tv, tile, 0)

    def dot1(s, j0, nj, sem, between):
        js = pl.ds(j0, nj)

        def to_sib(cols):
            return pltpu.make_async_remote_copy(
                src_ref=theirs(s, js, cols), dst_ref=sib_in.at[s, :, js, :, cols],
                send_sem=send_sem.at[sem], recv_sem=recv_sem.at[sem], device_id=sib, device_id_type=MESH,
            )

        def tile(n, carry):
            cols = pl.ds(pl.multiple_of(n * tn, tn), tn)
            share = jnp.dot(
                acts[s, :, js].reshape(4 * nj * hb, feats), w[:, cols], preferred_element_type=F32
            )
            part[s, :, js, :, cols] = share.astype(BF16).reshape(4, nj, hb, tn)
            to_sib(cols).start()
            return carry

        lax.fori_loop(0, hid // tn, tile, 0)
        between()
        to_sib(every).wait_recv()

        def own(way, carry):
            add_into(part.at[s, 2 * k + way, js], sib_in.at[s, way, js])
            return carry

        lax.fori_loop(0, 2, own, 0)

    mine = lambda s, way, j: part.at[s, 2 * k + way, j]
    to_z, back_z = (zp, zm), (zm, zp)
    hop = [[link(mine(0, way, j), z_in.at[way, 0, j], to_z[way]) for j in range(2)] for way in range(2)]
    both = pl.ds(0, 2)
    direct = [link(mine(1, way, both), z_in.at[1 - way, 1], back_z[way]) for way in range(2)]
    acc = [[link(mine(2, way, j), z_in.at[way, 2, j], to_z[way]) for j in range(2)] for way in range(2)]

    gx[0].start()
    load_w[0].wait()
    turn_w(0)
    gx[0].forward()
    gx[1].start()
    load_w[1].wait()
    turn_w(1)
    gx[0].finish()
    gy[0].start()
    load_w[2].wait()
    turn_w(2)
    gx[1].forward()
    gy[0].forward()
    load_w[3].wait()
    turn_w(3)
    gx[1].finish()
    gy[1].start()
    for load in load_w[4:]:
        load.wait()

    def half_step(u, carry):
        at_turn(u, 0, gy[0].finish)
        at_turn(u, 1, gy[1].finish)

        def between():
            at_turn(u, 0, gy[1].forward, gy[2].start)
            at_turn(u, 1, gy[2].forward, gy[3].start)

        dot1(0, u, 1, sib_first + u, between)
        for j in range(2):
            at_turn(u, j, hop[0][j].start, hop[1][j].start)
        return carry

    lax.fori_loop(0, 2, half_step, 0)

    def accumulate():
        def one(n, carry):
            j, way = lax.div(n, 2), lax.rem(n, 2)
            for i in range(4):
                at_turn(n, i, hop[i % 2][i // 2].wait_recv)
            add_into(part.at[2, 2 * k + way, pl.ds(j, 1)], z_in.at[way, 0, pl.ds(j, 1)])
            for i in range(4):
                at_turn(n, i, acc[i % 2][i // 2].start)
            return carry

        lax.fori_loop(0, 4, one, 0)

    def full_step(s, carry):
        for i in (1, 2, 3):
            at_turn(s, i, gy[1 + i].finish)

        def between():
            at_turn(s, 1, gy[3].forward, gy[4].start)
            at_turn(s, 2, gy[4].forward)

        dot1(s, 0, 2, sib_first + 1 + s, between)
        at_turn(s, 1, direct[0].start, direct[1].start)
        at_turn(s, 2, accumulate)
        return carry

    lax.fori_loop(1, 4, full_step, 0)
    load_og.wait()

    low, high, opp = nxt(z, 3), nxt(z, 1), nxt(z, 2)
    tokens_of = [(z, 0), (z, 1), (low, 0), (high, 0), (low, 1), (high, 1), (opp, 0), (opp, 1)]
    held_in = [(3, 3), (3, 3), (1, 2), (2, 1), (1, 2), (2, 1), (0, 0), (0, 0)]

    def turn(n, carry):
        cols = pl.ds(pl.multiple_of(n * tm, tm), tm)
        for t, steps in enumerate(held_in):
            rows = [acts[steps[b % 2], b, tokens_of[t][1], :, cols] for b in range(4)]
            acts_t[cols, t * 4 * hb:(t + 1) * 4 * hb] = jnp.concatenate(rows, axis=0).T
        return carry

    lax.fori_loop(0, feats // tm, turn, 0)

    def turn_rest(m, carry):
        turn_w(m)
        return carry

    lax.fori_loop(4, feats // tm, turn_rest, 0)

    piece = lambda zz, q: hidden.at[zz, 2 * k + q // 2, q % 2]
    own = [[link(piece(z, q), piece(z, q), to) for to in (sib, zp, zm)] for q in range(4)]
    fwd = [link(piece((low, high)[q // 2], q), piece((low, high)[q // 2], q), to_z[q // 2]) for q in range(4)]
    low_sib = [link(piece(low, q), piece(low, q), sib) for q in range(4)]
    high_sib = [link(piece(high, q), piece(high, q), sib) for q in range(4)]
    opp_sib = [link(piece(opp, q), piece(opp, q), sib) for q in range(4)]
    arrived(direct)

    def slope_piece(n, carry):
        j, way = lax.div(n, 2), lax.rem(n, 2)
        for i in range(4):
            at_turn(n, i, acc[i % 2][i // 2].wait_recv)
        start = pl.multiple_of((2 * way + j) * quarter, quarter)

        def tile(m, carry):
            cols = pl.ds(pl.multiple_of(m * tv, tv), tv)
            pre = part[3, 2 * k + way, j, :, cols].astype(F32)
            pre = pre + z_in[way, 2, j, :, cols].astype(F32) + z_in[1 - way, 1, j, :, cols].astype(F32)
            grad = og[pl.ds(start, quarter), cols].astype(F32) * gelu_slope(pre)
            hidden[z, 2 * k + way, j, :, cols] = grad.astype(BF16)
            return carry

        lax.fori_loop(0, hid // tv, tile, 0)
        for i in range(4):
            at_turn(n, i, *(copy.start for copy in own[2 * (i % 2) + i // 2]))
        return carry

    lax.fori_loop(0, 4, slope_piece, 0)

    def dot2(units):
        def tile(n, carry):
            cols = pl.ds(pl.multiple_of(n * tf, tf), tf)
            rows = [hidden[g, :, j].reshape(4 * hb, hid) for _, g, j in units]
            rows = rows[0] if len(rows) == 1 else jnp.concatenate(rows, axis=0)
            share = jnp.dot(rows, w_t[:, cols], preferred_element_type=F32).astype(BF16)
            for i, (s, _, j) in enumerate(units):
                ig[s, j, :, :, cols] = share[i * 4 * hb:(i + 1) * 4 * hb].reshape(4, hb, tf)
            return carry

        lax.fori_loop(0, feats // tf, tile, 0)

    def sum_into(out, terms):
        def tile(n, carry):
            cols = pl.ds(pl.multiple_of(n * tv, tv), tv)
            for p in range(out.shape[0]):
                for q in range(out.shape[1]):
                    total = terms[0][p, q, :, cols].astype(F32)
                    for term in terms[1:]:
                        total = total + term[p, q, :, cols].astype(F32)
                    out[p, q, :, cols] = total.astype(BF16)
            return carry

        lax.fori_loop(0, feats // tv, tile, 0)

    class ScatterY:
        def __init__(self, s0, ns, j0, nj):
            ss, js = pl.ds(s0, ns), pl.ds(j0, nj)
            self.blk = lambda by, rows: ig.at[ss, js, nxt(y, by), rows]
            self.im, self.ip = (lambda n: y_in_m.at[n, ss, js]), (lambda n: y_in_p.at[n, ss, js])
            self.out = lambda rows: xs.at[ss, js, rows]
            blk, im, ip = self.blk, self.im, self.ip
            self.op, self.om = link(blk(2, ha), im(0), yp), link(blk(2, hz), ip(0), ym)
            self.dp, self.dm = link(blk(1, hz), im(1), yp), link(blk(3, ha), ip(1), ym)
            self.ap, self.am = link(blk(1, ha), im(2), yp), link(blk(3, hz), ip(2), ym)

        def start(self):
            for copy in (self.op, self.om, self.dp, self.dm):
                copy.start()

        def middle(self):
            self.op.wait_recv()
            sum_into(self.blk(1, ha), [self.blk(1, ha), self.im(0)])
            self.ap.start()
            self.om.wait_recv()
            sum_into(self.blk(3, hz), [self.blk(3, hz), self.ip(0)])
            self.am.start()

        def finish(self):
            arrived((self.dp, self.dm, self.ap, self.am))
            sum_into(self.out(ha), [self.blk(0, ha), self.im(2), self.ip(1)])
            sum_into(self.out(hz), [self.blk(0, hz), self.im(1), self.ip(2)])

    class ReduceX:
        def __init__(self, s, g, j0, nj):
            one, js = pl.ds(s, 1), pl.ds(j0, nj)
            self.away = nxt(x, 4 - g)
            self.src = lambda rows: xs.at[one, js, rows]
            self.slot = lambda n: x_in.at[n, one, js]
            self.out = lambda rows: ig_ref.at[pl.ds(0, 1), js, rows]
            make = lambda rows, n, to: link(self.src(rows), self.slot(n), to, False)
            self.copies = (
                make(ha, 0, xp), make(hz, 0, xm), make(hz, 0, xp), make(ha, 1, xp), make(ha, 2, xm), make(hz, 3, xm)
            )

        def start(self):
            c = self.copies
            at_turn(self.away, 2, c[0].start, c[1].start)
            at_turn(self.away, 3, c[2].start)
            at_turn(self.away, 1, c[4].start)

        def middle(self):
            c, src, slot = self.copies, self.src, self.slot
            add = lambda rows: sum_into(src(rows), [src(rows), slot(0)])
            at_turn(self.away, 3, c[0].wait_recv, lambda: add(ha), c[3].start)
            at_turn(self.away, 1, c[1].wait_recv, lambda: add(hz), c[5].start)

        def finish(self):
            c, src, slot, out = self.copies, self.src, self.slot, self.out

            def total():
                arrived(c[2:])
                sum_into(out(ha), [src(ha), slot(1), slot(2)])
                sum_into(out(hz), [src(hz), slot(0), slot(3)])

            at_turn(self.away, 0, total)
            at_turn(self.away, 2, c[0].wait_send, c[1].wait_send)
            at_turn(self.away, 3, c[2].wait_send, c[3].wait_send)
            at_turn(self.away, 1, c[4].wait_send, c[5].wait_send)

    def dot3(rows_of, first, later, before):
        span = 16 * hb

        def tile(n, carry):
            before(n)
            cols = pl.ds(pl.multiple_of(n * t3, t3), t3)
            units = jnp.concatenate([hidden[g, :, j, :, cols].reshape(4 * hb, t3) for g, j in rows_of], axis=0)
            total = jnp.dot(acts_t[:, first:first + span], units, preferred_element_type=F32)
            if later:
                total = total + wg_ref[:, cols].astype(F32)
            wg_ref[:, cols] = total.astype(BF16)
            return carry

        lax.fori_loop(0, hid // t3, tile, 0)

    def neighbours(*qs):
        def work():
            for q in qs:
                own[q][1].wait_recv()
                if q < 2:
                    fwd[q].start()
                low_sib[q].start()
                own[q][2].wait_recv()
                if q >= 2:
                    fwd[q].start()
                high_sib[q].start()
        return work

    def opposite(*qs):
        def work():
            for q in qs:
                fwd[q].wait_recv()
                opp_sib[q].start()
        return work

    def from_sib(*copies):
        return lambda: arrived(copies)

    ys = [ScatterY(0, 1, 0, 2), ScatterY(1, 2, 0, 1), ScatterY(1, 2, 1, 1), ScatterY(3, 1, 0, 1), ScatterY(3, 1, 1, 1)]
    xr = [
        ReduceX(0, z, 0, 2), ReduceX(1, low, 0, 2), ReduceX(2, high, 0, 2), ReduceX(3, opp, 0, 1), ReduceX(3, opp, 1, 1)
    ]

    def early():
        def before(n):
            at_turn(n, 4, ys[1].middle, xr[0].middle, neighbours(1))
            at_turn(n, 8, ys[1].finish, neighbours(3))
            at_turn(n, 10, xr[0].finish)

        dot3(tokens_of[:4], 0, False, before)

    def batch(n, carry):
        other, j = lax.div(n + 1, 2), lax.div(n, 2)
        at_turn(n, 0, from_sib(*(own[q][0] for q in range(4))))
        at_turn(n, 1, neighbours(0, 2), ys[0].middle, from_sib(low_sib[0], low_sib[2], high_sib[0], high_sib[2]))
        at_turn(n, 2, from_sib(low_sib[1], low_sib[3], high_sib[1], high_sib[3]))
        dot2([(other, nxt(z, 3 * other), j), (2 * other, nxt(z, other), 1 - other + j)])
        at_turn(n, 0, ys[0].start)
        at_turn(n, 1, ys[1].start, ys[0].finish, xr[0].start, early)
        at_turn(n, 2, ys[2].start)
        return carry

    def last_batch(j, carry):
        at_turn(j, 0, opposite(0, 2), ys[2].middle, from_sib(opp_sib[0], opp_sib[2]))
        at_turn(
            j, 1, ys[2].finish, xr[1].start, xr[2].start, opposite(1, 3), ys[3].middle,
            from_sib(opp_sib[1], opp_sib[3]),
        )
        dot2([(3, opp, j)])
        at_turn(j, 0, ys[3].start)
        at_turn(j, 1, ys[4].start)
        return carry

    lax.fori_loop(0, 3, batch, 0)
    lax.fori_loop(0, 2, last_batch, 0)
    xr[1].middle()
    xr[2].middle()
    ys[3].finish()
    xr[3].start()

    def before_late(n):
        at_turn(n, 2, ys[4].middle, xr[3].middle)
        at_turn(n, 4, ys[4].finish, xr[4].start)
        at_turn(n, 6, xr[4].middle, xr[1].finish, xr[2].finish, xr[3].finish)

    dot3(tokens_of[4:], 16 * hb, True, before_late)
    xr[4].finish()

    for copy in made:
        if copy is not None:
            copy.wait_send()


def write_out(ig_ref, wg_ref, ig_out, wg_out, sem):
    rows = wg_ref.shape[0] // 4
    copies = [pltpu.make_async_copy(ig_ref, ig_out, sem.at[4])]
    for n in range(4):
        part = pl.ds(n * rows, rows)
        copies.append(pltpu.make_async_copy(wg_ref.at[part], wg_out.at[part], sem.at[n]))
    for copy in copies:
        copy.start()
    for copy in copies:
        copy.wait()


def per_device(acts, up_weight, out_grad):
    tb, feats = acts.shape
    ob, hid = out_grad.shape
    tokens = 16 * tb
    hb = tb // 2
    vmem = lambda *shape: pltpu.VMEM(shape, BF16)
    in_hbm = pl.BlockSpec(memory_space=pltpu.HBM)
    in_vmem = pl.BlockSpec(memory_space=pltpu.VMEM)
    flops = 3 * 2 * tokens * feats * hid
    acts, up_weight, out_grad = (
        pltpu.with_memory_space_constraint(a, pltpu.HBM) for a in (acts, up_weight, out_grad)
    )
    input_grad, weight_grad = pl.pallas_call(
        kernel,
        out_shape=(
            vmem(1, 2, hb, feats),
            vmem(feats, hid),
        ),
        in_specs=[in_hbm] * 3,
        out_specs=(in_vmem, in_vmem),
        scratch_shapes=[
            vmem(4, 4, 2, hb, feats),
            vmem(hid, feats),
            vmem(ob, hid),
            vmem(feats, tokens),
            vmem(4, 4, 2, hb, hid),
            vmem(4, 2, 2, hb, hid),
            vmem(2, 3, 2, hb, hid),
            vmem(4, 4, 2, hb, hid),
            vmem(4, 2, 4, hb, feats),
            vmem(3, 4, 2, hb // 2, feats),
            vmem(3, 4, 2, hb // 2, feats),
            vmem(4, 2, hb, feats),
            vmem(4, 4, 2, hb // 2, feats),
            pltpu.SemaphoreType.DMA((9,)),
            pltpu.SemaphoreType.DMA((N_SEMS,)),
            pltpu.SemaphoreType.DMA((N_SEMS,)),
        ],
        compiler_params=pltpu.CompilerParams(
            collective_id=0, has_side_effects=True, vmem_limit_bytes=50 * 2**20
        ),
        cost_estimate=pl.CostEstimate(flops=flops, bytes_accessed=4 * feats * hid, transcendentals=2 * ob * hid),
    )(acts, up_weight, out_grad)
    return pl.pallas_call(
        write_out,
        out_shape=(
            jax.ShapeDtypeStruct((tb, feats), BF16),
            jax.ShapeDtypeStruct((feats, hid), BF16),
        ),
        in_specs=[in_vmem] * 2,
        out_specs=(in_hbm, in_hbm),
        scratch_shapes=[pltpu.SemaphoreType.DMA((5,))],
        compiler_params=pltpu.CompilerParams(vmem_limit_bytes=2 * 2**20),
        cost_estimate=pl.CostEstimate(flops=0, bytes_accessed=2 * feats * hid, transcendentals=0),
    )(input_grad.reshape(tb, feats), weight_grad)


def solution(mesh):
    in_specs = (P("col", "row"), P("row", "col"), P("row", "col"))
    out_specs = (P("col", "row"), P("row", "col"))
    return jax.shard_map(
        per_device, mesh=mesh, in_specs=in_specs, out_specs=out_specs, check_vma=False
    )
```

time: 260 us -> 120 us (0.46)
  waiting for transfers between devices: 182 us -> 0 us
  Pallas kernels: 0 us -> 119 us
  matrix products: 45.6 us -> 0 us
  local copies, waits for them, and re-layouts: 14.5 us -> 0 us
  between operations: 13.8 us -> 0.64 us
  other arithmetic: 2.75 us -> 0 us
    pallas_call x0 -> x2, Pallas kernels: none -> 119 us  [the longest x1 115 us: per_device(): pl.pallas_call(kernel, out_shape=(vmem(1, 2, hb, feats), vmem(feats, hid)...]
    all_gather x2 -> x0, waiting for transfers between devices: 92.5 us -> none  [the longest x1 51.7 us: per_device(): all_acts = lax.all_gather(acts, 'col', axis=0, tiled=True)]
    reduce_scatter x2 -> x0, waiting for transfers between devices: 88.5 us -> none  [the longest x1 46 us: per_device(): lax.psum_scatter(lax.dot_general(part_rows, up_weight, (((1,), (1,)), (()...]
    dot_general x3 -> x0, matrix products: 45.6 us -> none  [the longest x1 15.6 us: per_device(): lax.dot_general(part_rows, up_weight, (((1,), (1,)), ((), ())), preferred...]
    unnamed x5 -> x0, local copies, waits for them, and re-layouts: 14.5 us -> none
    convert_element_type x1 -> x0, other arithmetic: 2.75 us -> none  [per_device(): (out_grad.astype(jnp.float32) * gelu_slope(pre_local)).astype(jnp.bfloat16)]
  transfers between devices with their start and end apart: 4 -> 0, of which waited for: 4 -> 0; matrix products, arithmetic and copies ran while one was open for 11% -> 0% of each run, Pallas kernels for 0% -> 0%
where the time goes in v7:
time: 120 us; the launch traced here: 119 us
  Pallas kernels  119 us (99%)
    pallas_call x1, Pallas kernels, per_device(): pl.pallas_call(kernel, out_shape=(vmem(1, 2, hb, feats), vmem(feats, hid)...  115 us
    pallas_call x1, Pallas kernels, per_device(): pl.pallas_call(write_out, out_shape=(jax.ShapeDtypeStruct((tb, feats), BF...  3.78 us

profile of v7, /device:TPU:2, one launch (start us, length us, event | category | flops | bytes accessed | tf_op | source)
XLA Modules:
  0.0 119.4 jit_solution(3241563879660965988)
XLA Ops:
  0.6 115.0 %shard_map.50 = (bf16[1,2,32,1536]{3,2,1,0:T(8,128)(2,1)S(1)}, bf16[1536,3072]{1,0:T(8,128)(2,1)S(1)}) custom-call(bf16[64,1536]{1,0:T(8,128)(2,1)} %acts_ref.1, bf16[1536,3072]{1,0:T(8,128)(2,1)} %w_ref.1, bf16[128,3072]{1,0:T(8,128)(2,1)} %og_ref.1), custom_call_target="tpu_custom_call" | custom-call | flops 28991029248 | bytes 18874368 | tf_op jit(solution)/shard_map/pallas_call | solution.py:503
  115.6 3.8 %shard_map.51 = (bf16[64,1536]{1,0:T(8,128)(2,1)}, bf16[1536,3072]{1,0:T(8,128)(2,1)}) custom-call(bf16[64,1536]{1,0:T(8,128)(2,1)S(1)} %bitcast.1, bf16[1536,3072]{1,0:T(8,128)(2,1)S(1)} %get-tuple-element.5.wg_ref), custom_call_target="tpu_custom_call" | custom-call | bytes 9437184 | tf_op jit(solution)/shard_map/pallas_call | solution.py:534

commit v8 on v5

--- a/solution.py
+++ b/solution.py
@@ -380,27 +380,17 @@
                 for n in used:
                     copies[n].wait_send()
 
-    def dot3(lo, hi, rows_of, first, later):
-        span = 16 * hb
-
+    blocks = hid // t3
+
+    def dot3(lo, hi):
         def tile(n, carry):
             cols = pl.ds(pl.multiple_of(n * t3, t3), t3)
-            units = jnp.concatenate([hidden[g, :, j, :, cols].reshape(4 * hb, t3) for g, j in rows_of], axis=0)
-            total = jnp.dot(acts_t[:, first:first + span], units, preferred_element_type=F32)
-            if later:
-                total = total + wg_ref[:, cols].astype(F32)
+            units = jnp.concatenate([hidden[g, :, j, :, cols].reshape(4 * hb, t3) for g, j in tokens_of], axis=0)
+            total = jnp.dot(acts_t[...], units, preferred_element_type=F32)
             wg_ref[:, cols] = total.astype(BF16)
             return carry
 
-        lax.fori_loop(lo, hi, tile, 0)
-
-    blocks = hid // t3
-
-    def early(lo, hi):
-        dot3(lo * blocks // 6, hi * blocks // 6, tokens_of[:4], 0, False)
-
-    def late(lo, hi):
-        dot3(lo * blocks // 6, hi * blocks // 6, tokens_of[4:], 16 * hb, True)
+        lax.fori_loop(lo * blocks // 6, hi * blocks // 6, tile, 0)
 
     def neighbours(qs):
         copies = []
@@ -440,45 +430,43 @@
     y1 = y_start(1, 2, 0, 1)
     y_finish(y0)
     x0 = x_start(0, z, 0, 2)
-    early(0, 2)
+    from_sib = neighbours((1, 3))
     y1 = y_middle(y1)
     x_middle(x0)
-    early(2, 6)
-    y_finish(y1)
-    from_sib = neighbours((1, 3))
-    x_finish(x0)
     arrived(from_sib)
     dot2([(1, low, (1,)), (2, high, (1,))])
     y2 = y_start(1, 2, 1, 1)
     from_sib = opposite((0, 2))
-    y2 = y_middle(y2)
+    y_finish(y1)
     arrived(from_sib)
     dot2([(3, opp, (0,))])
     y3 = y_start(3, 1, 0, 1)
+    y2 = y_middle(y2)
+    from_sib = opposite((1, 3))
+    x_finish(x0)
+    arrived(from_sib)
+    dot2([(3, opp, (1,))])
+    y4 = y_start(3, 1, 1, 1)
+    y3 = y_middle(y3)
     y_finish(y2)
     x1 = x_start(1, low, 0, 2)
     x2 = x_start(2, high, 0, 2)
-    from_sib = opposite((1, 3))
-    y3 = y_middle(y3)
-    arrived(from_sib)
-    dot2([(3, opp, (1,))])
-    y4 = y_start(3, 1, 1, 1)
+    dot3(0, 1)
+    y4 = y_middle(y4)
+    y_finish(y3)
+    x3 = x_start(3, opp, 0, 1)
     x_middle(x1)
     x_middle(x2)
-    y_finish(y3)
-    x3 = x_start(3, opp, 0, 1)
-    late(0, 1)
-    y4 = y_middle(y4)
-    x_middle(x3)
-    late(1, 2)
+    dot3(1, 2)
     y_finish(y4)
     x4 = x_start(3, opp, 1, 1)
-    late(2, 3)
+    x_middle(x3)
+    dot3(2, 3)
     x_middle(x4)
     x_finish(x1)
     x_finish(x2)
     x_finish(x3)
-    late(3, 6)
+    dot3(3, 6)
     x_finish(x4)
 
     for copy in sent:

time: 118 us -> 113 us (0.958)
  Pallas kernels: 117 us -> 113 us
    pallas_call x1, Pallas kernels: 114 us -> 109 us  [per_device(): pl.pallas_call(kernel, out_shape=(vmem(1, 2, hb, feats), vmem(feats, hid)...]
where the time goes in v8:
time: 113 us
  Pallas kernels  113 us (100%)
    pallas_call x1, Pallas kernels, per_device(): pl.pallas_call(kernel, out_shape=(vmem(1, 2, hb, feats), vmem(feats, hid)...  109 us
    pallas_call x1, Pallas kernels, per_device(): pl.pallas_call(write_out, out_shape=(jax.ShapeDtypeStruct((tb, feats), BF...  3.78 us

profile of v8, /device:TPU:2, one launch (start us, length us, event | category | flops | bytes accessed | tf_op | source)
XLA Modules:
  0.0 113.2 jit_solution(3282378472788868642)
XLA Ops:
  0.6 108.7 %shard_map.50 = (bf16[1,2,32,1536]{3,2,1,0:T(8,128)(2,1)S(1)}, bf16[1536,3072]{1,0:T(8,128)(2,1)S(1)}) custom-call(bf16[64,1536]{1,0:T(8,128)(2,1)} %acts_ref.1, bf16[1536,3072]{1,0:T(8,128)(2,1)} %w_ref.1, bf16[128,3072]{1,0:T(8,128)(2,1)} %og_ref.1), custom_call_target="tpu_custom_call" | custom-call | flops 28991029248 | bytes 18874368 | tf_op jit(solution)/shard_map/pallas_call | solution.py:501
  109.4 3.8 %shard_map.51 = (bf16[64,1536]{1,0:T(8,128)(2,1)}, bf16[1536,3072]{1,0:T(8,128)(2,1)}) custom-call(bf16[64,1536]{1,0:T(8,128)(2,1)S(1)} %bitcast.1, bf16[1536,3072]{1,0:T(8,128)(2,1)S(1)} %get-tuple-element.5.wg_ref), custom_call_target="tpu_custom_call" | custom-call | bytes 9437184 | tf_op jit(solution)/shard_map/pallas_call | solution.py:533

commit v9 on v8

--- a/solution.py
+++ b/solution.py
@@ -22,9 +22,15 @@
     return want if size % want == 0 else size
 
 
+def weight_block(acts_t, hidden, cols):
+    units = hidden[:, :, :, :, cols]
+    units = units.reshape(acts_t.shape[1], units.shape[-1])
+    return jnp.dot(acts_t[...], units, preferred_element_type=F32).astype(BF16)
+
+
 def kernel(
-    acts_ref, w_ref, og_ref, ig_ref, wg_ref,
-    acts, w_t, og, acts_t, part, sib_in, z_in_m, z_in_p, hidden, ig, y_in_m, y_in_p, xs, x_in,
+    acts_ref, w_ref, og_ref, ig_ref, wg_ref, acts_t, hidden,
+    acts, w_t, og, part, sib_in, z_in_m, z_in_p, ig, y_in_m, y_in_p, xs, x_in,
     local_sem, send_sem, recv_sem,
 ):
     tb, feats = acts_ref.shape
@@ -220,14 +226,13 @@
     load_og.wait()
 
     low, high, opp = nxt(z, 3), nxt(z, 1), nxt(z, 2)
-    tokens_of = [(z, 0), (z, 1), (low, 0), (high, 0), (low, 1), (high, 1), (opp, 0), (opp, 1)]
-    held_in = [(3, 3), (3, 3), (1, 2), (2, 1), (1, 2), (2, 1), (0, 0), (0, 0)]
+    held_in = [(z, 3, 3), (low, 1, 2), (high, 2, 1), (opp, 0, 0)]
 
     def turn(n, carry):
         cols = pl.ds(pl.multiple_of(n * tm, tm), tm)
-        for t, steps in enumerate(held_in):
-            rows = [acts[steps[b % 2], b, tokens_of[t][1], :, cols] for b in range(4)]
-            acts_t[cols, t * 4 * hb:(t + 1) * 4 * hb] = jnp.concatenate(rows, axis=0).T
+        for g, even, odd in held_in:
+            rows = [acts[(even, odd)[b % 2], b, :, :, cols].reshape(tb, tm) for b in range(4)]
+            acts_t[cols, pl.ds(pl.multiple_of(g * 4 * tb, 4 * tb), 4 * tb)] = jnp.concatenate(rows, axis=0).T
         return carry
 
     lax.fori_loop(0, feats // tm, turn, 0)
@@ -380,17 +385,15 @@
                 for n in used:
                     copies[n].wait_send()
 
-    blocks = hid // t3
+    blocks = hid // t3 * 3 // 4
 
     def dot3(lo, hi):
         def tile(n, carry):
             cols = pl.ds(pl.multiple_of(n * t3, t3), t3)
-            units = jnp.concatenate([hidden[g, :, j, :, cols].reshape(4 * hb, t3) for g, j in tokens_of], axis=0)
-            total = jnp.dot(acts_t[...], units, preferred_element_type=F32)
-            wg_ref[:, cols] = total.astype(BF16)
-            return carry
-
-        lax.fori_loop(lo * blocks // 6, hi * blocks // 6, tile, 0)
+            wg_ref[:, cols] = weight_block(acts_t, hidden, cols)
+            return carry
+
+        lax.fori_loop(lo * blocks // 9, hi * blocks // 9, tile, 0)
 
     def neighbours(qs):
         copies = []
@@ -451,22 +454,22 @@
     y_finish(y2)
     x1 = x_start(1, low, 0, 2)
     x2 = x_start(2, high, 0, 2)
-    dot3(0, 1)
+    dot3(0, 2)
     y4 = y_middle(y4)
     y_finish(y3)
     x3 = x_start(3, opp, 0, 1)
     x_middle(x1)
     x_middle(x2)
-    dot3(1, 2)
+    dot3(2, 4)
     y_finish(y4)
     x4 = x_start(3, opp, 1, 1)
     x_middle(x3)
-    dot3(2, 3)
+    dot3(4, 6)
     x_middle(x4)
     x_finish(x1)
     x_finish(x2)
     x_finish(x3)
-    dot3(3, 6)
+    dot3(6, 9)
     x_finish(x4)
 
     for copy in sent:
@@ -474,14 +477,21 @@
             copy.wait_send()
 
 
-def write_out(ig_ref, wg_ref, ig_out, wg_out, sem):
-    rows = wg_ref.shape[0] // 4
+def write_out(ig_ref, wg_ref, acts_t, hidden, ig_out, wg_out, stage, sem):
+    feats, width = stage.shape[1:]
+    done = wg_ref.shape[1] - stage.shape[0] * width
+    rows = feats // 4
     copies = [pltpu.make_async_copy(ig_ref, ig_out, sem.at[4])]
     for n in range(4):
-        part = pl.ds(n * rows, rows)
+        part = (pl.ds(n * rows, rows), pl.ds(0, done))
         copies.append(pltpu.make_async_copy(wg_ref.at[part], wg_out.at[part], sem.at[n]))
     for copy in copies:
         copy.start()
+    for n in range(stage.shape[0]):
+        cols = pl.ds(done + n * width, width)
+        stage[n] = weight_block(acts_t, hidden, cols)
+        copies.append(pltpu.make_async_copy(stage.at[n], wg_out.at[:, cols], sem.at[5 + n]))
+        copies[-1].start()
     for copy in copies:
         copy.wait()
 
@@ -495,27 +505,28 @@
     in_hbm = pl.BlockSpec(memory_space=pltpu.HBM)
     in_vmem = pl.BlockSpec(memory_space=pltpu.VMEM)
     flops = 3 * 2 * tokens * feats * hid
+    blocks = hid // tile_of(hid, 256)
     acts, up_weight, out_grad = (
         pltpu.with_memory_space_constraint(a, pltpu.HBM) for a in (acts, up_weight, out_grad)
     )
-    input_grad, weight_grad = pl.pallas_call(
+    input_grad, weight_grad, acts_t, hidden = pl.pallas_call(
         kernel,
         out_shape=(
             vmem(1, 2, hb, feats),
             vmem(feats, hid),
+            vmem(feats, tokens),
+            vmem(4, 4, 2, hb, hid),
         ),
         in_specs=[in_hbm] * 3,
-        out_specs=(in_vmem, in_vmem),
+        out_specs=(in_vmem,) * 4,
         scratch_shapes=[
             vmem(4, 4, 2, hb, feats),
             vmem(hid, feats),
             vmem(ob, hid),
-            vmem(feats, tokens),
             vmem(4, 4, 2, hb, hid),
             vmem(4, 2, 2, hb, hid),
             vmem(3, 2, hb, hid),
             vmem(3, 2, hb, hid),
-            vmem(4, 4, 2, hb, hid),
             vmem(4, 2, 4, hb, feats),
             vmem(3, 4, 2, hb // 2, feats),
             vmem(3, 4, 2, hb // 2, feats),
@@ -526,7 +537,7 @@
             pltpu.SemaphoreType.DMA((N_SEMS,)),
         ],
         compiler_params=pltpu.CompilerParams(
-            collective_id=0, has_side_effects=True, vmem_limit_bytes=50 * 2**20
+            collective_id=0, has_side_effects=True, vmem_limit_bytes=41 * 2**20
         ),
         cost_estimate=pl.CostEstimate(flops=flops, bytes_accessed=4 * feats * hid, transcendentals=2 * ob * hid),
     )(acts, up_weight, out_grad)
@@ -536,12 +547,12 @@
             jax.ShapeDtypeStruct((tb, feats), BF16),
             jax.ShapeDtypeStruct((feats, hid), BF16),
         ),
-        in_specs=[in_vmem] * 2,
+        in_specs=[in_vmem] * 4,
         out_specs=(in_hbm, in_hbm),
-        scratch_shapes=[pltpu.SemaphoreType.DMA((5,))],
-        compiler_params=pltpu.CompilerParams(vmem_limit_bytes=2 * 2**20),
-        cost_estimate=pl.CostEstimate(flops=0, bytes_accessed=2 * feats * hid, transcendentals=0),
-    )(input_grad.reshape(tb, feats), weight_grad)
+        scratch_shapes=[vmem(blocks // 4, feats, hid // blocks), pltpu.SemaphoreType.DMA((5 + blocks // 4,))],
+        compiler_params=pltpu.CompilerParams(vmem_limit_bytes=10 * 2**20),
+        cost_estimate=pl.CostEstimate(flops=flops // 12, bytes_accessed=2 * feats * hid, transcendentals=0),
+    )(input_grad.reshape(tb, feats), weight_grad, acts_t, hidden)
 
 
 def solution(mesh):

time: 113 us -> 113 us (level)
    pallas_call x1, Pallas kernels: 109 us -> 106 us  [per_device(): pl.pallas_call(kernel, out_shape=(vmem(1, 2, hb, feats), vmem(feats, hid)...]
    pallas_call x1, Pallas kernels: 3.78 us -> 5.75 us  [per_device(): pl.pallas_call(write_out, out_shape=(jax.ShapeDtypeStruct((tb, feats), BF...]
where the time goes in v9:
time: 113 us; the launch traced here: 112 us
  Pallas kernels  112 us (99%)
    pallas_call x1, Pallas kernels, per_device(): pl.pallas_call(kernel, out_shape=(vmem(1, 2, hb, feats), vmem(feats, hid)...  106 us
    pallas_call x1, Pallas kernels, per_device(): pl.pallas_call(write_out, out_shape=(jax.ShapeDtypeStruct((tb, feats), BF...  5.75 us

profile of v9, /device:TPU:2, one launch (start us, length us, event | category | flops | bytes accessed | tf_op | source)
XLA Modules:
  0.0 112.4 jit_solution(15311386122207743445)
XLA Ops:
  0.6 105.9 %shard_map.50 = (bf16[1,2,32,1536]{3,2,1,0:T(8,128)(2,1)S(1)}, bf16[1536,3072]{1,0:T(8,128)(2,1)S(1)}, bf16[1536,1024]{1,0:T(8,128)(2,1)S(1)}, bf16[4,4,2,32,3072]{4,3,2,1,0:T(8,128)(2,1)S(1)}) custom-call(bf16[64,1536]{1,0:T(8,128)(2,1)} %acts_ref.1, bf16[1536,3072]{1,0:T(8,128)(2,1)} %w_ref.1, bf16[128,3072]{1,0:T(8,128)(2,1)} %og_ref.1), custom_call_target="tpu_custom_call" | custom-call | flops 28991029248 | bytes 18874368 | tf_op jit(solution)/shard_map/pallas_call | solution.py:512
  106.5 5.8 %shard_map.51 = (bf16[64,1536]{1,0:T(8,128)(2,1)}, bf16[1536,3072]{1,0:T(8,128)(2,1)}) custom-call(bf16[64,1536]{1,0:T(8,128)(2,1)S(1)} %bitcast.1, bf16[1536,3072]{1,0:T(8,128)(2,1)S(1)} %get-tuple-element.7.wg_ref, bf16[1536,1024]{1,0:T(8,128)(2,1)S(1)} %get-tuple-element.8.acts_t, bf16[4,4,2,32,3072]{4,3,2,1,0:T(8,128)(2,1)S(1)} %get-tuple-element.9.hidden), custom_call_target="tpu_custom_call" | custom-call | flops 2415919104 | bytes 9437184 | tf_op jit(solution)/shard_map/pallas_call | solution.py:544

commit v10 on v9

--- a/solution.py
+++ b/solution.py
@@ -119,9 +119,8 @@
     def y_gather(s, j0, nj):
         return ag_start(lambda by, rows: acts.at[s, nxt(y, by), pl.ds(j0, nj), rows], yp, ym)
 
-    def turn_w(m, loaded=False):
-        if not loaded:
-            load_w[m].wait()
+    def turn_w(m):
+        load_w[m].wait()
 
         def tile(n, carry):
             cols = pl.ds(pl.multiple_of(n * tm, tm), tm)
@@ -183,8 +182,8 @@
     turn_w(3)
     ag_finish(gx1)
     g = y_gather(0, 1, 1)
-    for load in load_w[4:]:
-        load.wait()
+    for m in range(4, feats // tm):
+        turn_w(m)
     ag_finish(g0)
     opp_p, opp_m = [], []
     c = dot1(0, 0, 1)
@@ -235,10 +234,6 @@
             acts_t[cols, pl.ds(pl.multiple_of(g * 4 * tb, 4 * tb), 4 * tb)] = jnp.concatenate(rows, axis=0).T
         return carry
 
-    lax.fori_loop(0, feats // tm, turn, 0)
-    for m in range(4, feats // tm):
-        turn_w(m, True)
-
     dir_p.wait_recv()
     dir_m.wait_recv()
     piece = lambda zz, kk, q: hidden.at[zz, 2 * kk + q // 2, q % 2]
@@ -426,6 +421,7 @@
     arrived([own_sends[q][0] for q in arrivals])
     dot2([(0, z, (0, 1))])
     y0 = y_start(0, 1, 0, 2)
+    lax.fori_loop(0, feats // tm, turn, 0)
     from_sib = neighbours((0, 2))
     y0 = y_middle(y0)
     arrived(from_sib)

time: 113 us -> 111 us (0.982)
  Pallas kernels: 112 us -> 110 us
    pallas_call x1, Pallas kernels: 106 us -> 104 us  [per_device(): pl.pallas_call(kernel, out_shape=(vmem(1, 2, hb, feats), vmem(feats, hid)...]
where the time goes in v10:
time: 111 us
  Pallas kernels  110 us (99%)
    pallas_call x1, Pallas kernels, per_device(): pl.pallas_call(kernel, out_shape=(vmem(1, 2, hb, feats), vmem(feats, hid)...  104 us
    pallas_call x1, Pallas kernels, per_device(): pl.pallas_call(write_out, out_shape=(jax.ShapeDtypeStruct((tb, feats), BF...  5.75 us

profile of v10, /device:TPU:2, one launch (start us, length us, event | category | flops | bytes accessed | tf_op | source)
XLA Modules:
  0.0 110.8 jit_solution(14579916524900395023)
XLA Ops:
  0.6 104.3 %shard_map.50 = (bf16[1,2,32,1536]{3,2,1,0:T(8,128)(2,1)S(1)}, bf16[1536,3072]{1,0:T(8,128)(2,1)S(1)}, bf16[1536,1024]{1,0:T(8,128)(2,1)S(1)}, bf16[4,4,2,32,3072]{4,3,2,1,0:T(8,128)(2,1)S(1)}) custom-call(bf16[64,1536]{1,0:T(8,128)(2,1)} %acts_ref.1, bf16[1536,3072]{1,0:T(8,128)(2,1)} %w_ref.1, bf16[128,3072]{1,0:T(8,128)(2,1)} %og_ref.1), custom_call_target="tpu_custom_call" | custom-call | flops 28991029248 | bytes 18874368 | tf_op jit(solution)/shard_map/pallas_call | solution.py:508
  104.9 5.7 %shard_map.51 = (bf16[64,1536]{1,0:T(8,128)(2,1)}, bf16[1536,3072]{1,0:T(8,128)(2,1)}) custom-call(bf16[64,1536]{1,0:T(8,128)(2,1)S(1)} %bitcast.1, bf16[1536,3072]{1,0:T(8,128)(2,1)S(1)} %get-tuple-element.7.wg_ref, bf16[1536,1024]{1,0:T(8,128)(2,1)S(1)} %get-tuple-element.8.acts_t, bf16[4,4,2,32,3072]{4,3,2,1,0:T(8,128)(2,1)S(1)} %get-tuple-element.9.hidden), custom_call_target="tpu_custom_call" | custom-call | flops 2415919104 | bytes 9437184 | tf_op jit(solution)/shard_map/pallas_call | solution.py:540

commit v11 on v10

--- a/solution.py
+++ b/solution.py
@@ -188,24 +188,26 @@
     opp_p, opp_m = [], []
     c = dot1(0, 0, 1)
     g0 = ag_forward(g)
-    g = y_gather(1, 0, 2)
+    g = y_gather(1, 0, 1)
     core_sum(0, c, 0, 1)
     opp_p.append(send(mine(0, 0).at[0], z_in_m.at[0, 0], zp))
     opp_m.append(send(mine(0, 1).at[0], z_in_p.at[0, 0], zm))
     ag_finish(g0)
     c = dot1(0, 1, 1)
     g0 = ag_forward(g)
-    g = y_gather(2, 0, 2)
+    g = y_gather(1, 1, 1)
     core_sum(0, c, 1, 1)
     opp_p.append(send(mine(0, 0).at[1], z_in_m.at[0, 1], zp))
     opp_m.append(send(mine(0, 1).at[1], z_in_p.at[0, 1], zm))
-    ag_finish(g0)
-    c = dot1(1, 0, 2)
-    g0 = ag_forward(g)
-    g = y_gather(3, 0, 2)
-    core_sum(1, c, 0, 2)
-    dir_p = send(mine(1, 1), z_in_m.at[1], zp)
-    dir_m = send(mine(1, 0), z_in_p.at[1], zm)
+    dir_p, dir_m = [], []
+    for j in range(2):
+        ag_finish(g0)
+        c = dot1(1, j, 1)
+        g0 = ag_forward(g)
+        g = y_gather(2 + j, 0, 2)
+        core_sum(1, c, j, 1)
+        dir_p.append(send(mine(1, 1).at[j], z_in_m.at[1, j], zp))
+        dir_m.append(send(mine(1, 0).at[j], z_in_p.at[1, j], zm))
     ag_finish(g0)
     c = dot1(2, 0, 2)
     g0 = ag_forward(g)
@@ -234,8 +236,8 @@
             acts_t[cols, pl.ds(pl.multiple_of(g * 4 * tb, 4 * tb), 4 * tb)] = jnp.concatenate(rows, axis=0).T
         return carry
 
-    dir_p.wait_recv()
-    dir_m.wait_recv()
+    for copy in (*dir_p, *dir_m):
+        copy.wait_recv()
     piece = lambda zz, kk, q: hidden.at[zz, 2 * kk + q // 2, q % 2]
 
     def slope_piece(q, from_m, from_p):

time: 111 us -> 114 us (1.027)
  Pallas kernels: 110 us -> 113 us
    pallas_call x1, Pallas kernels: 104 us -> 107 us  [per_device(): pl.pallas_call(kernel, out_shape=(vmem(1, 2, hb, feats), vmem(feats, hid)...]
where the time goes in v11:
time: 114 us
  Pallas kernels  113 us (99%)
    pallas_call x1, Pallas kernels, per_device(): pl.pallas_call(kernel, out_shape=(vmem(1, 2, hb, feats), vmem(feats, hid)...  107 us
    pallas_call x1, Pallas kernels, per_device(): pl.pallas_call(write_out, out_shape=(jax.ShapeDtypeStruct((tb, feats), BF...  5.75 us

profile of v11, /device:TPU:2, one launch (start us, length us, event | category | flops | bytes accessed | tf_op | source)
XLA Modules:
  0.0 113.9 jit_solution(13888305059563026635)
XLA Ops:
  0.6 107.3 %shard_map.50 = (bf16[1,2,32,1536]{3,2,1,0:T(8,128)(2,1)S(1)}, bf16[1536,3072]{1,0:T(8,128)(2,1)S(1)}, bf16[1536,1024]{1,0:T(8,128)(2,1)S(1)}, bf16[4,4,2,32,3072]{4,3,2,1,0:T(8,128)(2,1)S(1)}) custom-call(bf16[64,1536]{1,0:T(8,128)(2,1)} %acts_ref.1, bf16[1536,3072]{1,0:T(8,128)(2,1)} %w_ref.1, bf16[128,3072]{1,0:T(8,128)(2,1)} %og_ref.1), custom_call_target="tpu_custom_call" | custom-call | flops 28991029248 | bytes 18874368 | tf_op jit(solution)/shard_map/pallas_call | solution.py:510
  107.9 5.7 %shard_map.51 = (bf16[64,1536]{1,0:T(8,128)(2,1)}, bf16[1536,3072]{1,0:T(8,128)(2,1)}) custom-call(bf16[64,1536]{1,0:T(8,128)(2,1)S(1)} %bitcast.1, bf16[1536,3072]{1,0:T(8,128)(2,1)S(1)} %get-tuple-element.7.wg_ref, bf16[1536,1024]{1,0:T(8,128)(2,1)S(1)} %get-tuple-element.8.acts_t, bf16[4,4,2,32,3072]{4,3,2,1,0:T(8,128)(2,1)S(1)} %get-tuple-element.9.hidden), custom_call_target="tpu_custom_call" | custom-call | flops 2415919104 | bytes 9437184 | tf_op jit(solution)/shard_map/pallas_call | solution.py:542

commit v12 on v10

--- a/solution.py
+++ b/solution.py
@@ -185,20 +185,15 @@
     for m in range(4, feats // tm):
         turn_w(m)
     ag_finish(g0)
-    opp_p, opp_m = [], []
-    c = dot1(0, 0, 1)
     g0 = ag_forward(g)
     g = y_gather(1, 0, 2)
-    core_sum(0, c, 0, 1)
-    opp_p.append(send(mine(0, 0).at[0], z_in_m.at[0, 0], zp))
-    opp_m.append(send(mine(0, 1).at[0], z_in_p.at[0, 0], zm))
     ag_finish(g0)
-    c = dot1(0, 1, 1)
+    c = dot1(0, 0, 2)
     g0 = ag_forward(g)
     g = y_gather(2, 0, 2)
-    core_sum(0, c, 1, 1)
-    opp_p.append(send(mine(0, 0).at[1], z_in_m.at[0, 1], zp))
-    opp_m.append(send(mine(0, 1).at[1], z_in_p.at[0, 1], zm))
+    core_sum(0, c, 0, 2)
+    opp_p = [send(mine(0, 0).at[j], z_in_m.at[0, j], zp) for j in range(2)]
+    opp_m = [send(mine(0, 1).at[j], z_in_p.at[0, j], zm) for j in range(2)]
     ag_finish(g0)
     c = dot1(1, 0, 2)
     g0 = ag_forward(g)

time: 111 us -> 113 us (1.018)
  Pallas kernels: 110 us -> 113 us
    pallas_call x1, Pallas kernels: 104 us -> 107 us  [per_device(): pl.pallas_call(kernel, out_shape=(vmem(1, 2, hb, feats), vmem(feats, hid)...]
where the time goes in v12:
time: 113 us
  Pallas kernels  113 us (100%)
    pallas_call x1, Pallas kernels, per_device(): pl.pallas_call(kernel, out_shape=(vmem(1, 2, hb, feats), vmem(feats, hid)...  107 us
    pallas_call x1, Pallas kernels, per_device(): pl.pallas_call(write_out, out_shape=(jax.ShapeDtypeStruct((tb, feats), BF...  5.75 us

profile of v12, /device:TPU:2, one launch (start us, length us, event | category | flops | bytes accessed | tf_op | source)
XLA Modules:
  0.0 113.4 jit_solution(11296422176141305185)
XLA Ops:
  0.6 106.8 %shard_map.50 = (bf16[1,2,32,1536]{3,2,1,0:T(8,128)(2,1)S(1)}, bf16[1536,3072]{1,0:T(8,128)(2,1)S(1)}, bf16[1536,1024]{1,0:T(8,128)(2,1)S(1)}, bf16[4,4,2,32,3072]{4,3,2,1,0:T(8,128)(2,1)S(1)}) custom-call(bf16[64,1536]{1,0:T(8,128)(2,1)} %acts_ref.1, bf16[1536,3072]{1,0:T(8,128)(2,1)} %w_ref.1, bf16[128,3072]{1,0:T(8,128)(2,1)} %og_ref.1), custom_call_target="tpu_custom_call" | custom-call | flops 28991029248 | bytes 18874368 | tf_op jit(solution)/shard_map/pallas_call | solution.py:503
  107.5 5.7 %shard_map.51 = (bf16[64,1536]{1,0:T(8,128)(2,1)}, bf16[1536,3072]{1,0:T(8,128)(2,1)}) custom-call(bf16[64,1536]{1,0:T(8,128)(2,1)S(1)} %bitcast.1, bf16[1536,3072]{1,0:T(8,128)(2,1)S(1)} %get-tuple-element.7.wg_ref, bf16[1536,1024]{1,0:T(8,128)(2,1)S(1)} %get-tuple-element.8.acts_t, bf16[4,4,2,32,3072]{4,3,2,1,0:T(8,128)(2,1)S(1)} %get-tuple-element.9.hidden), custom_call_target="tpu_custom_call" | custom-call | flops 2415919104 | bytes 9437184 | tf_op jit(solution)/shard_map/pallas_call | solution.py:535
